TPU v7x, 32 devices: a whole 2x2x4 slice. The times are simulated.
32 devices in a mesh: dp: 8 (over z, y), mp: 4 (over x, core).
Axes of the slice: x: 2, y: 2, z: 4, core: 2. Of those that a mesh axis runs over, the one named last changes fastest.
Arguments:
- tokens: bfloat16 [4096, 768], P(('dp', 'mp')), may hold values from -6 to 6
- teacher: bfloat16 [4096, 768], P(('dp', 'mp')), may hold values from -6 to 6
- segments: int32 [4096], P('dp'), may hold values from 0 to 31, never falling along the last dimension, each value on 1 to 512 neighbouring positions
- valid_mask: int32 [4096], P('dp'), may hold values from 0 to 1, as said below
- routes: int32 [4096, 2], P('dp'), may hold values from 0 to 15, all different within a row; in each aligned block of 512 rows (0 to 511, 512 to 1023, ...) at most 128 rows name the same one
- first_gain: float32 [768], replicated, may hold values from 0.5 to 1.5
- second_gain: float32 [768], replicated, may hold values from 0.5 to 1.5
- router_weight: float32 [768, 16], replicated, may hold values from -0.21875 to 0.21875
- attention_in: float32 [768, 3, 768], P('dp', None, 'mp'), may hold values from -0.21875 to 0.21875
- attention_out: float32 [768, 768], P('dp', 'mp'), may hold values from -1.25 to 1.25
- dense_in: float32 [768, 2, 2048], P('dp', None, 'mp'), may hold values from -0.21875 to 0.21875
- dense_out: float32 [768, 2048], P('dp', 'mp'), may hold values from -0.125 to 0.125
- expert_in: float32 [16, 768, 2, 2048], P('dp', None, None, 'mp'), may hold values from -0.21875 to 0.21875
- expert_out: float32 [16, 768, 2048], P('dp', None, 'mp'), may hold values from -0.125 to 0.125
- moment_first_gain: float32 [768], replicated, may hold values from -192 to 192
- moment_second_gain: float32 [768], replicated, may hold values from -192 to 192
- moment_router: float32 [768, 16], replicated, may hold values from -21760 to 21760
- moment_attention_in: float32 [768, 3, 768], P('dp', None, 'mp'), may hold values from -21760 to 21760
- moment_attention_out: float32 [768, 768], P('dp', 'mp'), may hold values from -80 to 80
- moment_dense_in: float32 [768, 2, 2048], P('dp', None, 'mp'), may hold values from -80 to 80
- moment_dense_out: float32 [768, 2048], P('dp', 'mp'), may hold values from -80 to 80
- moment_expert_in: float32 [16, 768, 2, 2048], P('dp', None, None, 'mp'), may hold values from -14 to 14
- moment_expert_out: float32 [16, 768, 2048], P('dp', None, 'mp'), may hold values from -14 to 14
Outputs:
- output: bfloat16 [4096, 768], P(('dp', 'mp'))
- loss_value: float32 [], replicated
- grad_tokens: float32 [4096, 768], P(('dp', 'mp'))
- grad_first_gain: float32 [768], replicated
- grad_second_gain: float32 [768], replicated
- grad_router: float32 [768, 16], replicated
- grad_attention_in: float32 [768, 3, 768], P('dp', None, 'mp')
- grad_attention_out: float32 [768, 768], P('dp', 'mp')
- grad_dense_in: float32 [768, 2, 2048], P('dp', None, 'mp')
- grad_dense_out: float32 [768, 2048], P('dp', 'mp')
- grad_expert_in: float32 [16, 768, 2, 2048], P('dp', None, None, 'mp')
- grad_expert_out: float32 [16, 768, 2048], P('dp', None, 'mp')
- new_moment_first_gain: float32 [768], replicated
- new_moment_second_gain: float32 [768], replicated
- new_moment_router: float32 [768, 16], replicated
- new_moment_attention_in: float32 [768, 3, 768], P('dp', None, 'mp')
- new_moment_attention_out: float32 [768, 768], P('dp', 'mp')
- new_moment_dense_in: float32 [768, 2, 2048], P('dp', None, 'mp')
- new_moment_dense_out: float32 [768, 2048], P('dp', 'mp')
- new_moment_expert_in: float32 [16, 768, 2, 2048], P('dp', None, None, 'mp')
- new_moment_expert_out: float32 [16, 768, 2048], P('dp', None, 'mp')
- step_first_gain: float32 [768], replicated
- step_second_gain: float32 [768], replicated
- new_router: float32 [768, 16], replicated
- new_attention_in: float32 [768, 3, 768], P('dp', None, 'mp')
- step_attention_out: float32 [768, 768], P('dp', 'mp')
- new_dense_in: float32 [768, 2, 2048], P('dp', None, 'mp')
- new_dense_out: float32 [768, 2048], P('dp', 'mp')
- new_expert_in: float32 [16, 768, 2, 2048], P('dp', None, None, 'mp')
- new_expert_out: float32 [16, 768, 2048], P('dp', None, 'mp')
Inputs may be any that keep to these rules, and one draw needn't show every extreme that they name: `valid_mask`: within each sequence of 512 tokens, valid tokens come first and padding follows. `routes`: A token names two different experts; within the 512 rows of one sequence no expert is named more than 128 times.
All inputs are finite; a program needn't handle non-finite values.
Results may differ from a plain program's by a relative error of at most 0.017.
Values may be sent and summed in bfloat16 or wider, within the bound.
No kernel may reach another device: no remote copies, remote signals or barrier semaphores. Data moves between devices by JAX's collectives and lax.ppermute only.
A program may use at most 256 MiB of HBM per device.

v0:
```python
import jax
import jax.numpy as jnp
from jax import lax
from jax.sharding import PartitionSpec as P

D = 768
HEADS = 12
HEAD_DIM = 64
FF = 2048
NS_ITERS = 2


highest = lax.Precision.HIGHEST
norm_eps = 1e-06
rope_base = 10000.0
masked_score = -1e30
ns_first = 3.4445
ns_second = -4.775
ns_third = 2.0315
decay_rate = 0.5
gain_rate = 0.05
router_rate = 0.02


def rms_scale(values):
    return lax.rsqrt(jnp.mean(values * values, axis=-1, keepdims=True) + norm_eps)


def rotate(values, positions, direction):
    half_dim = values.shape[-1] // 2
    frequency = rope_base ** (-jnp.arange(half_dim, dtype=jnp.float32) * 2.0 / values.shape[-1])
    angles = positions[:, None] * frequency[None, :]
    cosine = jnp.cos(angles)[:, None, :]
    sine_part = direction * jnp.sin(angles)[:, None, :]
    first_half = values[..., :half_dim]
    second = values[..., half_dim:]
    return jnp.concatenate(
        [first_half * cosine - second * sine_part, second * cosine + first_half * sine_part],
        axis=-1,
    )


def slot_tables(route_rows, expert_total, capacity):
    flat_routes = route_rows.reshape(-1)
    assign_count = flat_routes.shape[0]
    sort_order = jnp.argsort(flat_routes, stable=True)
    onehot = (flat_routes[:, None] == jnp.arange(expert_total, dtype=jnp.int32)[None, :]).astype(
        jnp.int32
    )
    counts = jnp.sum(onehot, axis=0)
    starts = jnp.cumsum(counts) - counts
    sorted_ranks = jnp.arange(assign_count, dtype=jnp.int32) - starts[flat_routes[sort_order]]
    slot_ranks = jnp.zeros((assign_count,), jnp.int32).at[sort_order].set(sorted_ranks)
    slot_ids = flat_routes * capacity + slot_ranks
    source = (
        jnp.full((expert_total * capacity,), -1, jnp.int32)
        .at[slot_ids]
        .set(jnp.arange(assign_count, dtype=jnp.int32))
    )
    return (slot_ids, source)


def swiglu_back(gate_up, grad_inner):
    gate_values = gate_up[..., 0, :]
    up_values = gate_up[..., 1, :]
    sigmoid_gate = jax.nn.sigmoid(gate_values)
    grad_gate_part = (
        grad_inner * up_values * sigmoid_gate * (1.0 + gate_values * (1.0 - sigmoid_gate))
    )
    grad_up_part = grad_inner * gate_values * sigmoid_gate
    return jnp.stack([grad_gate_part, grad_up_part], axis=-2)


def norm_back(grad_normed, inputs, row_scale, norm_gain):
    scaled = grad_normed * norm_gain
    grad_gain = jnp.sum(grad_normed * inputs * row_scale, axis=0)
    grad_inputs = row_scale * scaled - inputs * row_scale**3 * jnp.mean(
        scaled * inputs, axis=-1, keepdims=True
    )
    return (grad_inputs, grad_gain)


def gather_rows(values):
    return lax.all_gather(values, "mp", axis=0, tiled=True)


def scatter_rows(values):
    return lax.psum_scatter(values, "mp", scatter_dimension=0, tiled=True)


def send_owner(values):
    return lax.all_to_all(values, "dp", split_axis=0, concat_axis=0, tiled=True)


def send_source(values):
    return lax.all_to_all(values, "dp", split_axis=0, concat_axis=0, tiled=True)


def allowed_block(segments, block_start, block_rows):
    seq_len = segments.shape[0]
    query_index = block_start + jnp.arange(block_rows)
    key_index = jnp.arange(seq_len)
    return (segments[:, None] == segments[None, :]) & (query_index[:, None] >= key_index[None, :])


def attention_forward(queries, key_rows, value_rows, segments):
    seq_len = queries.shape[0]
    block_rows = min(512, seq_len)

    def one_block(block_start):
        allowed = allowed_block(segments, block_start, block_rows)
        scores = jnp.einsum("qhd,khd->hqk", queries, key_rows, preferred_element_type=jnp.float32)
        scores = jnp.where(allowed[None], scores, masked_score)
        row_peak = jnp.max(scores, axis=-1, keepdims=True)
        exponent = jnp.exp(scores - row_peak)
        row_total = jnp.sum(exponent, axis=-1, keepdims=True)
        score_weights = (exponent / row_total).astype(jnp.bfloat16)
        mixed_heads = jnp.einsum(
            "hqk,khd->qhd", score_weights, value_rows, preferred_element_type=jnp.float32
        )
        return (mixed_heads, (row_peak + jnp.log(row_total))[:, :, 0])

    block_starts = jnp.arange(seq_len // block_rows) * block_rows
    mixed_heads, log_totals = lax.map(one_block, block_starts)
    return (mixed_heads.reshape(seq_len, queries.shape[1], queries.shape[2]), log_totals)


def attention_backward(queries, key_rows, value_rows, segments, log_totals, grad_mixed):
    seq_len = queries.shape[0]
    block_rows = min(512, seq_len)

    def one_block(running, step_inputs):
        grad_keys, grad_values = running
        block_start, block_totals = step_inputs
        allowed = allowed_block(segments, block_start, block_rows)
        scores = jnp.einsum("qhd,khd->hqk", queries, key_rows, preferred_element_type=jnp.float32)
        scores = jnp.where(allowed[None], scores, masked_score)
        score_weights = jnp.exp(scores - block_totals[:, :, None])
        grad_weights = jnp.einsum(
            "qhd,khd->hqk", grad_mixed, value_rows, preferred_element_type=jnp.float32
        )
        row_dots = jnp.sum(grad_weights * score_weights, axis=-1, keepdims=True)
        grad_scores = (score_weights * (grad_weights - row_dots)).astype(jnp.bfloat16)
        grad_query = jnp.einsum(
            "hqk,khd->qhd", grad_scores, key_rows, preferred_element_type=jnp.float32
        )
        grad_keys = grad_keys + jnp.einsum(
            "hqk,qhd->khd", grad_scores, queries, preferred_element_type=jnp.float32
        )
        grad_values = grad_values + jnp.einsum(
            "hqk,qhd->khd",
            score_weights.astype(jnp.bfloat16),
            grad_mixed,
            preferred_element_type=jnp.float32,
        )
        return ((grad_keys, grad_values), grad_query)

    block_starts = jnp.arange(seq_len // block_rows) * block_rows
    zero_rows = jnp.zeros(key_rows.shape, jnp.float32)
    (grad_keys, grad_values), grad_queries = lax.scan(
        one_block, (zero_rows, zero_rows), (block_starts, log_totals)
    )
    return (grad_queries.reshape(queries.shape), grad_keys, grad_values)


def gram_term(matrix):
    return jnp.einsum("dc,ec->de", matrix, matrix, preferred_element_type=jnp.float32)


def normed_delta(moment, step_rate):
    return -step_rate * moment * lax.rsqrt(jnp.mean(moment * moment) + 1e-12)


def local(
    tokens,
    teacher,
    segments,
    valid_mask,
    routes,
    first_gain,
    second_gain,
    router_weight,
    attention_in,
    attention_out,
    dense_in,
    dense_out,
    expert_in,
    expert_out,
    moment_first_gain,
    moment_second_gain,
    moment_router,
    moment_attention_in,
    moment_attention_out,
    moment_dense_in,
    moment_dense_out,
    moment_expert_in,
    moment_expert_out,
):
    row_count, model_width = tokens.shape
    mp_ways = lax.axis_size("mp")
    dp_ways = lax.axis_size("dp")
    mp_place = lax.axis_index("mp")
    dp_place = lax.axis_index("dp")
    seq_len = row_count * mp_ways
    expert_total = router_weight.shape[1]
    capacity = 4 * seq_len // expert_total
    shard_rows = attention_in.shape[0]
    slab_count = expert_in.shape[0]
    sharing = FF // (expert_in.shape[3] * mp_ways)
    project_scale = (3 * HEADS * HEAD_DIM / D) ** 0.5
    mix_scale = (HEADS * HEAD_DIM / D) ** 0.5
    pair_scale = (2 * FF / D) ** 0.5
    single_scale = (FF / D) ** 0.5
    slab_pair_scale = (2 * FF / (sharing * D)) ** 0.5
    slab_single_scale = (FF / (sharing * D)) ** 0.5
    mask_float = valid_mask.astype(jnp.float32)
    valid_count = lax.psum(jnp.sum(mask_float), "dp")
    own_mask = lax.dynamic_slice_in_dim(mask_float, mp_place * row_count, row_count, 0)
    weight_project, weight_mix, weight_gate_up, weight_down = (
        lax.all_gather(attention_in.astype(jnp.bfloat16), "dp", axis=0, tiled=True),
        lax.all_gather(attention_out.astype(jnp.bfloat16), "dp", axis=0, tiled=True),
        lax.all_gather(dense_in.astype(jnp.bfloat16), "dp", axis=0, tiled=True),
        lax.all_gather(dense_out.astype(jnp.bfloat16), "dp", axis=0, tiled=True),
    )
    router_low = router_weight.astype(jnp.bfloat16)
    expert_gate_up = expert_in.astype(jnp.bfloat16).reshape(slab_count, model_width, -1)
    expert_down = expert_out.astype(jnp.bfloat16)
    token_float = tokens.astype(jnp.float32)
    scale_one = rms_scale(token_float)
    full_one = gather_rows((token_float * scale_one * first_gain).astype(jnp.bfloat16))
    projected = jnp.dot(
        full_one, weight_project.reshape(model_width, -1), preferred_element_type=jnp.float32
    )
    projected = projected.reshape(seq_len, 3, -1, HEAD_DIM)
    positions = jnp.arange(seq_len, dtype=jnp.float32)
    query_scale = HEAD_DIM ** (-0.5)
    queries = (rotate(projected[:, 0], positions, 1.0) * query_scale).astype(jnp.bfloat16)
    key_rows = rotate(projected[:, 1], positions, 1.0).astype(jnp.bfloat16)
    value_rows = projected[:, 2].astype(jnp.bfloat16)
    mixed_heads, log_totals = attention_forward(queries, key_rows, value_rows, segments)
    mixed_low = mixed_heads.reshape(seq_len, -1).astype(jnp.bfloat16)
    attended = scatter_rows(
        jnp.einsum("sh,dh->sd", mixed_low, weight_mix, preferred_element_type=jnp.float32)
    )
    hidden = token_float + attended
    scale_two = rms_scale(hidden)
    full_two = gather_rows((hidden * scale_two * second_gain).astype(jnp.bfloat16))
    gate_up = jnp.dot(
        full_two, weight_gate_up.reshape(model_width, -1), preferred_element_type=jnp.float32
    ).reshape(seq_len, 2, -1)
    dense_inner = (jax.nn.silu(gate_up[:, 0]) * gate_up[:, 1]).astype(jnp.bfloat16)
    dense_part = jnp.einsum(
        "sf,df->sd", dense_inner, weight_down, preferred_element_type=jnp.float32
    )
    logits = jnp.dot(full_two, router_low, preferred_element_type=jnp.float32)
    onehot = routes[:, :, None] == jnp.arange(expert_total, dtype=jnp.int32)[None, None, :]
    chosen = jnp.sum(jnp.where(onehot, logits[:, None, :], 0.0), axis=-1)
    gate_probs = jax.nn.softmax(chosen, axis=-1)
    slot_ids, source = slot_tables(routes, expert_total, capacity)
    filled = source >= 0
    source_clip = jnp.maximum(source, 0)
    source_rows = source_clip // 2
    dispatched = jnp.where(filled[:, None], full_two[source_rows], jnp.zeros((), jnp.bfloat16))
    spread_rows = jnp.broadcast_to(
        dispatched.reshape(expert_total, 1, capacity, model_width),
        (expert_total, sharing, capacity, model_width),
    )
    received = send_owner(
        spread_rows.reshape(expert_total * sharing, capacity, model_width)
    ).reshape(dp_ways, slab_count, capacity, model_width)
    expert_hidden = jnp.einsum(
        "alcd,ldk->alck", received, expert_gate_up, preferred_element_type=jnp.float32
    ).reshape(dp_ways, slab_count, capacity, 2, -1)
    expert_inner = (jax.nn.silu(expert_hidden[..., 0, :]) * expert_hidden[..., 1, :]).astype(
        jnp.bfloat16
    )
    expert_part = jnp.einsum(
        "alcf,ldf->alcd", expert_inner, expert_down, preferred_element_type=jnp.float32
    ).astype(jnp.bfloat16)
    returned = send_source(expert_part.reshape(dp_ways * slab_count, capacity, model_width))
    expert_rows = jnp.sum(
        returned.reshape(expert_total, sharing, capacity, model_width).astype(jnp.float32), axis=1
    ).reshape(-1, model_width)
    picked = expert_rows[slot_ids].reshape(seq_len, 2, model_width)
    mixture = jnp.sum(gate_probs[:, :, None] * picked, axis=1)
    branch = scatter_rows(dense_part + mixture)
    output = hidden + branch
    errors = output - teacher.astype(jnp.float32)
    loss_local = jnp.sum(jnp.sum(errors * errors, axis=-1) * own_mask)
    factor = seq_len * dp_ways / valid_count
    grad_output = errors * (own_mask * factor)[:, None]
    grad_branch = gather_rows(grad_output.astype(jnp.bfloat16))
    back_project, back_mix, back_gate_up, back_down = (
        weight_project,
        weight_mix,
        weight_gate_up,
        weight_down,
    )
    grad_dense_inner = jnp.einsum(
        "sd,df->sf", grad_branch, back_down, preferred_element_type=jnp.float32
    )
    grad_down = jnp.einsum(
        "sd,sf->df", grad_branch, dense_inner, preferred_element_type=jnp.float32
    )
    grad_gate_up = swiglu_back(gate_up, grad_dense_inner).reshape(seq_len, -1).astype(jnp.bfloat16)
    grad_dense_in = jnp.einsum(
        "sd,sk->dk", full_two, grad_gate_up, preferred_element_type=jnp.float32
    )
    grad_full_two = jnp.einsum(
        "sk,dk->sd",
        grad_gate_up,
        back_gate_up.reshape(model_width, -1),
        preferred_element_type=jnp.float32,
    )
    grad_chosen_raw = jnp.einsum(
        "sd,skd->sk", grad_branch.astype(jnp.float32), picked, precision=highest
    )
    grad_chosen = gate_probs * (
        grad_chosen_raw - jnp.sum(gate_probs * grad_chosen_raw, axis=-1, keepdims=True)
    )
    grad_logits = jnp.sum(jnp.where(onehot, grad_chosen[:, :, None], 0.0), axis=1)
    grad_router = jnp.einsum(
        "sd,se->de", full_two.astype(jnp.float32), grad_logits, precision=highest
    )
    grad_full_two = grad_full_two + jnp.einsum(
        "se,de->sd", grad_logits, router_low.astype(jnp.float32), precision=highest
    )
    gate_flat = gate_probs.reshape(-1)
    grad_slots = jnp.where(
        filled[:, None],
        gate_flat[source_clip][:, None] * grad_branch[source_rows].astype(jnp.float32),
        0.0,
    ).astype(jnp.bfloat16)
    spread_grads = jnp.broadcast_to(
        grad_slots.reshape(expert_total, 1, capacity, model_width),
        (expert_total, sharing, capacity, model_width),
    )
    grad_received = send_owner(
        spread_grads.reshape(expert_total * sharing, capacity, model_width)
    ).reshape(dp_ways, slab_count, capacity, model_width)
    grad_expert_inner = jnp.einsum(
        "alcd,ldf->alcf", grad_received, expert_down, preferred_element_type=jnp.float32
    )
    grad_expert_down = jnp.einsum(
        "alcd,alcf->ldf", grad_received, expert_inner, preferred_element_type=jnp.float32
    )
    grad_expert_hidden = (
        swiglu_back(expert_hidden, grad_expert_inner)
        .reshape(dp_ways, slab_count, capacity, -1)
        .astype(jnp.bfloat16)
    )
    grad_expert_gate_up = jnp.einsum(
        "alcd,alck->ldk", received, grad_expert_hidden, preferred_element_type=jnp.float32
    )
    grad_dispatch = jnp.einsum(
        "alck,ldk->alcd", grad_expert_hidden, expert_gate_up, preferred_element_type=jnp.float32
    ).astype(jnp.bfloat16)
    grad_returned = send_source(grad_dispatch.reshape(dp_ways * slab_count, capacity, model_width))
    grad_slot_rows = jnp.sum(
        grad_returned.reshape(expert_total, sharing, capacity, model_width).astype(jnp.float32),
        axis=1,
    ).reshape(-1, model_width)
    grad_full_two = grad_full_two + jnp.sum(
        grad_slot_rows[slot_ids].reshape(seq_len, 2, model_width), axis=1
    )
    grad_normed_two = scatter_rows(grad_full_two)
    grad_hidden, grad_second = norm_back(grad_normed_two, hidden, scale_two, second_gain)
    grad_hidden = grad_hidden + grad_output
    grad_attended = gather_rows(grad_hidden.astype(jnp.bfloat16))
    grad_mix = jnp.einsum("sd,sh->dh", grad_attended, mixed_low, preferred_element_type=jnp.float32)
    grad_mixed = (
        jnp.einsum("sd,dh->sh", grad_attended, back_mix, preferred_element_type=jnp.float32)
        .astype(jnp.bfloat16)
        .reshape(mixed_heads.shape)
    )
    grad_queries, grad_keys, grad_values = attention_backward(
        queries, key_rows, value_rows, segments, log_totals, grad_mixed
    )
    grad_projected = jnp.stack(
        [
            rotate(grad_queries * query_scale, positions, -1.0),
            rotate(grad_keys, positions, -1.0),
            grad_values,
        ],
        axis=1,
    )
    grad_projected = grad_projected.reshape(seq_len, -1).astype(jnp.bfloat16)
    grad_project = jnp.einsum(
        "sd,sk->dk", full_one, grad_projected, preferred_element_type=jnp.float32
    )
    grad_full_one = jnp.einsum(
        "sk,dk->sd",
        grad_projected,
        back_project.reshape(model_width, -1),
        preferred_element_type=jnp.float32,
    )
    grad_normed_one = scatter_rows(grad_full_one)
    grad_tokens, grad_first = norm_back(grad_normed_one, token_float, scale_one, first_gain)
    grad_tokens = grad_tokens + grad_hidden
    shard_project, shard_mix, shard_gate_up, shard_down = (
        lax.psum_scatter(
            grad_project.reshape(model_width, 3, -1), "dp", scatter_dimension=0, tiled=True
        ),
        lax.psum_scatter(grad_mix, "dp", scatter_dimension=0, tiled=True),
        lax.psum_scatter(
            grad_dense_in.reshape(model_width, 2, -1), "dp", scatter_dimension=0, tiled=True
        ),
        lax.psum_scatter(grad_down, "dp", scatter_dimension=0, tiled=True),
    )
    router_total, first_total, second_total, loss_total = lax.psum(
        (grad_router, grad_first, grad_second, loss_local), ("dp", "mp")
    )
    loss_value = loss_total / (valid_count * model_width)
    grad_expert_in = grad_expert_gate_up.reshape(expert_in.shape)
    new_moment_first = decay_rate * moment_first_gain + first_total
    new_moment_second = decay_rate * moment_second_gain + second_total
    new_moment_router = decay_rate * moment_router + router_total
    new_moment_project = decay_rate * moment_attention_in + shard_project
    new_moment_mix = decay_rate * moment_attention_out + shard_mix
    new_moment_gate_up = decay_rate * moment_dense_in + shard_gate_up
    new_moment_down = decay_rate * moment_dense_out + shard_down
    new_moment_expert_in = decay_rate * moment_expert_in + grad_expert_in
    new_moment_expert_out = decay_rate * moment_expert_out + grad_expert_down
    full_project, full_mix, full_gate_up, full_down = (
        lax.all_gather(new_moment_project.astype(jnp.bfloat16), "dp", axis=0, tiled=True),
        lax.all_gather(new_moment_mix.astype(jnp.bfloat16), "dp", axis=0, tiled=True),
        lax.all_gather(new_moment_gate_up.astype(jnp.bfloat16), "dp", axis=0, tiled=True),
        lax.all_gather(new_moment_down.astype(jnp.bfloat16), "dp", axis=0, tiled=True),
    )
    matrices = [
        full_project.reshape(model_width, -1),
        full_mix,
        full_gate_up.reshape(model_width, -1),
        full_down,
    ]
    for slab_index in range(slab_count):
        matrices.append(
            new_moment_expert_in[slab_index].astype(jnp.bfloat16).reshape(model_width, -1)
        )
        matrices.append(new_moment_expert_out[slab_index].astype(jnp.bfloat16))
    square_parts = jnp.stack(
        [jnp.sum(jnp.square(matrix.astype(jnp.float32))) for matrix in matrices]
    )
    square_sums = lax.psum(square_parts, "mp")
    current = [
        (matrix.astype(jnp.float32) * lax.rsqrt(square_sums[index] + 1e-12)).astype(jnp.bfloat16)
        for index, matrix in enumerate(matrices)
    ]
    iterates = [matrix.astype(jnp.float32) for matrix in current]
    for iteration in range(NS_ITERS):
        gram_stack = lax.psum(
            jnp.stack(
                [gram_term(matrix).astype(jnp.bfloat16).astype(jnp.float32) for matrix in current]
            ).astype(jnp.bfloat16),
            "mp",
        ).astype(jnp.float32)
        iterates = []
        for index, matrix in enumerate(current):
            gram_total = gram_stack[index]
            gram_low = gram_total.astype(jnp.bfloat16)
            square = jnp.dot(gram_low, gram_low, preferred_element_type=jnp.float32)
            polynomial = (ns_second * gram_total + ns_third * square).astype(jnp.bfloat16)
            iterates.append(
                ns_first * matrix.astype(jnp.float32)
                + jnp.dot(polynomial, matrix, preferred_element_type=jnp.float32)
            )
        current = [iterate_value.astype(jnp.bfloat16) for iterate_value in iterates]

    def own_rows(full_matrix, shape):
        return lax.dynamic_slice_in_dim(full_matrix, dp_place * shard_rows, shard_rows, 0).reshape(
            shape
        )

    step_first = normed_delta(new_moment_first, gain_rate)
    step_second = normed_delta(new_moment_second, gain_rate)
    new_router = router_weight + normed_delta(new_moment_router, router_rate)
    new_attention_in = attention_in + -project_scale * own_rows(iterates[0], attention_in.shape)
    step_mix = -mix_scale * own_rows(iterates[1], attention_out.shape)
    new_dense_in = dense_in + -pair_scale * own_rows(iterates[2], dense_in.shape)
    new_dense_out = dense_out + -single_scale * own_rows(iterates[3], dense_out.shape)
    expert_in_steps = jnp.stack([iterates[4 + 2 * slab_index] for slab_index in range(slab_count)])
    expert_out_steps = jnp.stack([iterates[5 + 2 * slab_index] for slab_index in range(slab_count)])
    new_expert_in = expert_in + -slab_pair_scale * expert_in_steps.reshape(expert_in.shape)
    new_expert_out = expert_out + -slab_single_scale * expert_out_steps
    return (
        output.astype(jnp.bfloat16),
        loss_value,
        grad_tokens,
        first_total,
        second_total,
        router_total,
        shard_project,
        shard_mix,
        shard_gate_up,
        shard_down,
        grad_expert_in,
        grad_expert_down,
        new_moment_first,
        new_moment_second,
        new_moment_router,
        new_moment_project,
        new_moment_mix,
        new_moment_gate_up,
        new_moment_down,
        new_moment_expert_in,
        new_moment_expert_out,
        step_first,
        step_second,
        new_router,
        new_attention_in,
        step_mix,
        new_dense_in,
        new_dense_out,
        new_expert_in,
        new_expert_out,
    )


def solution(mesh):
    return jax.shard_map(
        local,
        mesh=mesh,
        in_specs=(
            P(("dp", "mp"), None),
            P(("dp", "mp"), None),
            P("dp"),
            P("dp"),
            P("dp", None),
            P(),
            P(),
            P(),
            P("dp", None, "mp"),
            P("dp", "mp"),
            P("dp", None, "mp"),
            P("dp", "mp"),
            P("dp", None, None, "mp"),
            P("dp", None, "mp"),
            P(),
            P(),
            P(),
            P("dp", None, "mp"),
            P("dp", "mp"),
            P("dp", None, "mp"),
            P("dp", "mp"),
            P("dp", None, None, "mp"),
            P("dp", None, "mp"),
        ),
        out_specs=(
            P(("dp", "mp"), None),
            P(),
            P(("dp", "mp"), None),
            P(),
            P(),
            P(),
            P("dp", None, "mp"),
            P("dp", "mp"),
            P("dp", None, "mp"),
            P("dp", "mp"),
            P("dp", None, None, "mp"),
            P("dp", None, "mp"),
            P(),
            P(),
            P(),
            P("dp", None, "mp"),
            P("dp", "mp"),
            P("dp", None, "mp"),
            P("dp", "mp"),
            P("dp", None, None, "mp"),
            P("dp", None, "mp"),
            P(),
            P(),
            P(),
            P("dp", None, "mp"),
            P("dp", "mp"),
            P("dp", None, "mp"),
            P("dp", "mp"),
            P("dp", None, None, "mp"),
            P("dp", None, "mp"),
        ),
        check_vma=False,
    )
```

profile of v0, /device:TPU:0, one launch (start us, length us, event | category | flops | bytes accessed | tf_op | source)
XLA Modules:
  0.0 1564.5 jit_solution(4803523766812451776)
XLA Ops:
  13.7 34.8 %all_gather.38 = bf16[768,192]{1,0:T(8,128)(2,1)} all-gather(bf16[96,192]{1,0:T(8,128)(2,1)S(1)} %convert_element_type.601), channel_id=1, replica_groups=mesh['dp'=8,'mp'=4] {'dp'}, dimensions={0}, use_global_device_ids=true | all-gather | bytes 331776 | tf_op jit(solution)/shard_map/all_gather | solution.py:221
  49.6 8.6 all_gather.36
  58.2 39.1 %all_gather.37 = bf16[768,3,192]{2,1,0:T(4,128)(2,1)S(1)} all-gather(bf16[96,3,192]{2,1,0:T(4,128)(2,1)S(1)} %copy.253), channel_id=1, replica_groups=mesh['dp'=8,'mp'=4] {'dp'}, dimensions={0}, use_global_device_ids=true | all-gather | bytes 995328 | tf_op jit(solution)/shard_map/all_gather | solution.py:220
  135.6 7.6 all_gather.39
  143.2 9.4 gather_fusion.1
  160.5 6.6 convert_element_type.608
  173.2 58.8 %all-to-all-done = bf16[16,128,768]{2,1,0:T(8,128)(2,1)} async-done(((bf16[16,128,768]{2,1,0:T(8,128)(2,1)}), bf16[16,128,768]{2,1,0:T(8,128)(2,1)}, u32[]{:S(2)}, u32[]{:S(2)}) %all-to-all-start) | async-done | bytes 3145760 | tf_op jit(solution)/shard_map/all_to_all | solution.py:92
  232.0 9.5 convolution_bitcast_fusion
  241.6 11.7 reshape.580
  253.3 10.1 fusion.295
  276.9 112.5 %all_gather.41 = bf16[768,512]{1,0:T(8,128)(2,1)} all-gather(bf16[96,512]{1,0:T(8,128)(2,1)S(1)} %convert_element_type.605), channel_id=1, replica_groups=mesh['dp'=8,'mp'=4] {'dp'}, dimensions={0}, use_global_device_ids=true | all-gather | bytes 884736 | tf_op jit(solution)/shard_map/all_gather | solution.py:223
  399.9 8.6 gather_fusion.2
  413.6 16.2 %multiply_reduce_fusion.1 = f32[512,768]{1,0:T(8,128)S(1)} fusion(f32[512,2,768]{2,1,0:T(2,128)} %reshape.584, f32[512,2]{1,0:T(8,128)S(1)} %copy.258), kind=kLoop, calls=%fused_computation.62 | loop fusion | flops 1179648 | bytes 4722688 | tf_op jit(solution)/shard_map/reduce_sum | solution.py:285
  432.9 20.4 %psum.57 = f32[]{:T(128)} all-reduce(f32[]{:T(128)} %convert_reduce_fusion.1), channel_id=1, replica_groups=mesh['dp'=8,'mp'=4] {'dp'}, use_global_device_ids=true, to_apply=%region_19.20 | all-reduce | flops 1 | bytes 8 | tf_op jit(solution)/shard_map/psum | solution.py:217
  455.0 9.7 gather_fusion.4
  465.8 8.6 all_gather.42
  474.4 9.4 gather_fusion.5
  498.6 90.1 %all-to-all-done.2 = bf16[16,128,768]{2,1,0:T(8,128)(2,1)} async-done(((bf16[16,128,768]{2,1,0:T(8,128)(2,1)}), bf16[16,128,768]{2,1,0:T(8,128)(2,1)}, u32[]{:S(2)}, u32[]{:S(2)}) %all-to-all-start.2) | async-done | bytes 3145760 | tf_op jit(solution)/shard_map/all_to_all | solution.py:92
  588.8 8.3 fusion.43
  605.6 7.3 convert_bitcast_fusion
  621.3 6.8 gather_fusion.3
  640.3 62.3 %all-to-all-done.3 = bf16[16,128,768]{2,1,0:T(8,128)(2,1)} async-done(((bf16[16,128,768]{2,1,0:T(8,128)(2,1)}), bf16[16,128,768]{2,1,0:T(8,128)(2,1)}, u32[]{:S(2)}, u32[]{:S(2)}) %all-to-all-start.3) | async-done | bytes 3145760 | tf_op jit(solution)/shard_map/all_to_all | solution.py:96
  707.7 8.6 gather_fusion.6
  735.1 20.8 %reduce-scatter.15.cloned.1.call-done = f32[128,768]{1,0:T(8,128)} async-done(((f32[512,768]{1,0:T(8,128)}), f32[128,768]{1,0:T(8,128)}) %reduce-scatter.15.cloned.1.call-update) | async-done | bytes 393232 | tf_op jit(solution)/shard_map/reduce_scatter | solution.py:88
  759.3 8.2 all_gather.43
  782.4 33.7 %all_gather.47 = bf16[768,512]{1,0:T(8,128)(2,1)S(1)} all-gather(bf16[96,512]{1,0:T(8,128)(2,1)S(1)} %copy-done.78), channel_id=1, replica_groups=mesh['dp'=8,'mp'=4] {'dp'}, dimensions={0}, use_global_device_ids=true | all-gather | bytes 884736 | tf_op jit(solution)/shard_map/all_gather | solution.py:428
  818.0 6.6 copy.268
  824.6 6.5 multiply_add_fusion.2
  838.5 7.0 bitcast_add_fusion
  852.5 26.8 %reduce-scatter.19.cloned.1.call-done = f32[96,192]{1,0:T(8,128)} async-done(((f32[768,192]{1,0:T(8,128)}), f32[96,192]{1,0:T(8,128)}) %reduce-scatter.19.cloned.1.call-update) | async-done | bytes 73744 | tf_op jit(solution)/shard_map/reduce_scatter | solution.py:404
  880.8 31.9 %all_gather.45 = bf16[768,192]{1,0:T(8,128)(2,1)S(1)} all-gather(bf16[96,192]{1,0:T(8,128)(2,1)S(1)} %get-tuple-element.289), channel_id=1, replica_groups=mesh['dp'=8,'mp'=4] {'dp'}, dimensions={0}, use_global_device_ids=true | all-gather | bytes 331776 | tf_op jit(solution)/shard_map/all_gather | solution.py:426
  914.2 36.2 %reduce-scatter.25.cloned.1.call-done = f32[96,576]{1,0:T(8,128)} async-done(((f32[768,576]{1,0:T(8,128)}), f32[96,576]{1,0:T(8,128)}) %reduce-scatter.25.cloned.1.call-update) | async-done | bytes 221200
  952.4 36.2 %all_gather.44 = bf16[768,3,192]{2,1,0:T(4,128)(2,1)S(1)} all-gather(bf16[96,3,192]{2,1,0:T(4,128)(2,1)S(1)} %copy.284), channel_id=1, replica_groups=mesh['dp'=8,'mp'=4] {'dp'}, dimensions={0}, use_global_device_ids=true | all-gather | bytes 995328 | tf_op jit(solution)/shard_map/all_gather | solution.py:425
  1044.1 153.1 %all-reduce.4.cloned.1.call-done = bf16[8,768,768]{2,1,0:T(8,128)(2,1)} async-done(((bf16[8,768,768]{2,1,0:T(8,128)(2,1)}), bf16[8,768,768]{2,1,0:T(8,128)(2,1)}) %all-reduce.4.cloned.1.call-update) | async-done | bytes 9437200 | tf_op jit(solution)/shard_map/psum | solution.py:451
  1197.2 12.4 convert_element_type.667
  1221.2 7.2 add_convert_fusion.2
  1228.3 7.1 add_convert_fusion.1
  1260.7 7.5 add_convert_fusion
  1283.2 10.5 copy.299
  1293.8 9.3 reshape.592
  1307.8 41.4 %all-reduce = (f32[]{:T(128)}, f32[768]{0:T(1024)S(1)}, f32[768]{0:T(1024)S(1)}, f32[768,16]{0,1:T(8,128)S(1)}) all-reduce(f32[]{:T(128)} %multiply_reduce_fusion.9, f32[768]{0:T(1024)S(1)} %get-tuple-element.269, f32[768]{0:T(1024)S(1)} %get-tuple-element.267, f32[768,16]{0,1:T(8,128)S(1)} %fusion.304), channel_id=1, replica_groups=mesh['dp'=8,'mp'=4] {'dp','mp'}, use_global_device_ids=true, to_apply=%region_17.18 | all-reduce | flops 13825 | bytes 110600 | tf_op jit(solution)/shard_map/psum | solution.py:410
  1359.3 93.8 %all-reduce.6.cloned.1.call-done = bf16[8,768,768]{2,1,0:T(8,128)(2,1)} async-done(((bf16[8,768,768]{2,1,0:T(8,128)(2,1)}), bf16[8,768,768]{2,1,0:T(8,128)(2,1)}) %all-reduce.6.cloned.1.call-update) | async-done | bytes 9437200 | tf_op jit(solution)/shard_map/psum | solution.py:451
  1453.1 11.8 convert_element_type.719
  1483.1 8.1 multiply_add_fusion
  1491.2 7.3 multiply_add_fusion.1
  1504.6 6.6 fusion.161
  1511.2 7.2 fusion.184
  1547.0 9.0 fusion
  (469 shorter events, 365.2 us)
Async XLA Ops:
  8.0 125.8 %reduce-scatter.11.cloned.1.call-start = ((), (), s32[]{:S(2)}) async-start(), calls=%async_computation.12 | async-start | bytes 1966080 | tf_op jit(solution)/shard_map/reduce_scatter | solution.py:88
  9.7 48.5 %copy-start.108 = (f32[128]{0:T(128)}, f32[128]{0:T(128)S(1)}, u32[]{:S(2)}) copy-start(f32[128]{0:T(128)S(1)} %get-tuple-element.343) | copy-start | bytes 1540
  13.7 87.1 %copy-start.19 = (pred[512,512]{0,1:T(8,128)(4,1)}, pred[512,512]{0,1:T(8,128)(4,1)S(1)}, u32[]{:S(2)}) copy-start(pred[512,512]{0,1:T(8,128)(4,1)S(1)} %fusion.154) | copy-start | bytes 786436
  58.2 40.7 %copy-start.17 = (bf16[512,768]{1,0:T(8,128)(2,1)}, bf16[512,768]{1,0:T(8,128)(2,1)S(1)}, u32[]{:S(2)}) copy-start(bf16[512,768]{1,0:T(8,128)(2,1)S(1)} %all_gather.36) | copy-start | bytes 2359300
  103.9 29.9 %copy-start.29 = (bf16[128,768]{1,0:T(8,128)(2,1)S(1)}, bf16[128,768]{1,0:T(8,128)(2,1)}, u32[]{:S(2)}) copy-start(bf16[128,768]{1,0:T(8,128)(2,1)} %param.23) | copy-start | bytes 589828
  108.4 27.0 %copy-start.91 = (f32[768]{0:T(1024)S(1)}, f32[768]{0:T(1024)}, u32[]{:S(2)}) copy-start(f32[768]{0:T(1024)} %param.29) | copy-start | bytes 9220
  143.2 351.7 %copy-start = (bf16[512,768]{1,0:T(8,128)(2,1)}, bf16[512,768]{1,0:T(8,128)(2,1)S(1)}, u32[]{:S(2)}) copy-start(bf16[512,768]{1,0:T(8,128)(2,1)S(1)} %all_gather.39) | copy-start | bytes 2359300
  155.9 76.1 %all-to-all-start = ((bf16[16,128,768]{2,1,0:T(8,128)(2,1)}), bf16[16,128,768]{2,1,0:T(8,128)(2,1)}, u32[]{:S(2)}, u32[]{:S(2)}) async-start(bf16[16,128,768]{2,1,0:T(8,128)(2,1)} %broadcast_select_fusion), calls=%async_computation.1 | async-start | bytes 6291456 | tf_op jit(solution)/shard_map/all_to_all | solution.py:92
  271.4 123.4 %all-to-all-start.1 = ((bf16[16,128,768]{2,1,0:T(8,128)(2,1)}), bf16[16,128,768]{2,1,0:T(8,128)(2,1)}, u32[]{:S(2)}, u32[]{:S(2)}) async-start(bf16[16,128,768]{2,1,0:T(8,128)(2,1)} %bitcast.593), calls=%async_computation.2 | async-start | bytes 6291456 | tf_op jit(solution)/shard_map/all_to_all | solution.py:96
  276.0 113.4 %all-gather.3.cloned.1.call-start = ((), (), s32[]{:S(2)}) async-start(), calls=%async_computation.13 | async-start | bytes 1769472 | tf_op jit(solution)/shard_map/all_gather | solution.py:222
  276.8 114.3 %copy-start.75 = (f32[768,16]{0,1:T(8,128)S(1)}, f32[768,16]{0,1:T(8,128)}, u32[]{:S(2)}) copy-start(f32[768,16]{0,1:T(8,128)} %param.30) | copy-start | bytes 147460
  276.8 187.9 %reduce-scatter.13.cloned.1.call-start = ((), (), s32[]{:S(2)}) async-start(), calls=%async_computation.14 | async-start | bytes 1966080 | tf_op jit(solution)/shard_map/reduce_scatter | solution.py:88
  455.0 19.5 %copy-start.87 = (s32[2048]{0:T(1024)S(1)}, s32[2048]{0:T(1024)}, u32[]{:S(2)}) copy-start(s32[2048]{0:T(1024)} %copy-done.86) | copy-start | bytes 24580
  487.4 101.4 %all-to-all-start.2 = ((bf16[16,128,768]{2,1,0:T(8,128)(2,1)}), bf16[16,128,768]{2,1,0:T(8,128)(2,1)}, u32[]{:S(2)}, u32[]{:S(2)}) async-start(bf16[16,128,768]{2,1,0:T(8,128)(2,1)} %fusion.2), calls=%async_computation.4 | async-start | bytes 6291456 | tf_op jit(solution)/shard_map/all_to_all | solution.py:92
  491.9 239.4 %reduce-scatter.21.cloned.1.call-start = ((), (), s32[]{:S(2)}) async-start(), calls=%async_computation.18 | async-start | bytes 3538944 | tf_op jit(solution)/shard_map/reduce_scatter | solution.py:405
  614.7 87.9 %all-to-all-start.3 = ((bf16[16,128,768]{2,1,0:T(8,128)(2,1)}), bf16[16,128,768]{2,1,0:T(8,128)(2,1)}, u32[]{:S(2)}, u32[]{:S(2)}) async-start(bf16[16,128,768]{2,1,0:T(8,128)(2,1)} %bitcast.592), calls=%async_computation.5 | async-start | bytes 6291456 | tf_op jit(solution)/shard_map/all_to_all | solution.py:96
  619.2 114.2 %reduce-scatter.23.cloned.1.call-start = ((), (), s32[]{:S(2)}) async-start(), calls=%async_computation.19 | async-start | bytes 1769472 | tf_op jit(solution)/shard_map/reduce_scatter | solution.py:408
  621.1 134.8 %reduce-scatter.15.cloned.1.call-start = ((), (), s32[]{:S(2)}) async-start(), calls=%async_computation.15 | async-start | bytes 1966080 | tf_op jit(solution)/shard_map/reduce_scatter | solution.py:88
  729.3 26.6 %copy-start.33 = (f32[128,768]{1,0:T(8,128)S(1)}, f32[128,768]{1,0:T(8,128)}, u32[]{:S(2)}) copy-start(f32[128,768]{1,0:T(8,128)} %reduce-scatter.13.cloned.1.call-done) | copy-start | bytes 1179652
  729.3 26.6 %copy-start.50 = (bf16[128,768]{1,0:T(8,128)(2,1)S(1)}, bf16[128,768]{1,0:T(8,128)(2,1)}, u32[]{:S(2)}) copy-start(bf16[128,768]{1,0:T(8,128)(2,1)} %param.24) | copy-start | bytes 589828
  729.3 26.6 %copy-start.92 = (f32[768]{0:T(1024)S(1)}, f32[768]{0:T(1024)}, u32[]{:S(2)}) copy-start(f32[768]{0:T(1024)} %param.29) | copy-start | bytes 9220
  729.3 26.6 %copy-start.114 = (f32[128]{0:T(128)S(1)}, f32[128]{0:T(128)}, u32[]{:S(2)}) copy-start(f32[128]{0:T(128)} %copy-done.113) | copy-start | bytes 1540
  729.4 27.8 %copy-start.111 = (f32[128]{0:T(128)S(1)}, f32[128]{0:T(128)}, u32[]{:S(2)}) copy-start(f32[128]{0:T(128)} %copy-done.110) | copy-start | bytes 1540
  729.4 27.8 %copy-start.120 = (f32[128]{0:T(128)S(1)}, f32[128]{0:T(128)}, u32[]{:S(2)}) copy-start(f32[128]{0:T(128)} %get-tuple-element.347) | copy-start | bytes 1540
  729.4 120.2 %all-gather.5.cloned.1.call-start = ((), (), s32[]{:S(2)}) async-start(), calls=%async_computation.20 | async-start | bytes 1769472 | tf_op jit(solution)/shard_map/all_gather | solution.py:427
  733.3 146.0 %reduce-scatter.19.cloned.1.call-start = ((), (), s32[]{:S(2)}) async-start(), calls=%async_computation.17 | async-start | bytes 884736 | tf_op jit(solution)/shard_map/reduce_scatter | solution.py:404
  775.6 174.8 %reduce-scatter.25.cloned.1.call-start = ((), (), s32[]{:S(2)}) async-start(), calls=%async_computation.23 | async-start | bytes 2211840
  782.3 414.9 %all-reduce.4.cloned.1.call-start = ((), (), s32[]{:S(2)}) async-start(), calls=%async_computation.21 | async-start | bytes 18874368 | tf_op jit(solution)/shard_map/psum | solution.py:451
  848.2 31.1 %copy-start.84 = (f32[96,192]{1,0:T(8,128)S(1)}, f32[96,192]{1,0:T(8,128)}, u32[]{:S(2)}) copy-start(f32[96,192]{1,0:T(8,128)} %param.41) | copy-start | bytes 221188
  849.6 101.9 %copy-start.61 = (f32[96,3,192]{0,2,1:T(8,128)S(1)}, f32[96,3,192]{0,2,1:T(8,128)}, u32[]{:S(2)}) copy-start(f32[96,3,192]{0,2,1:T(8,128)} %copy.280) | copy-start | bytes 663556
  989.5 20.6 %slice-start = ((s8[6291456]{0:T(1024)(128)(4,1)}), s8[2097152]{0:T(1024)(128)(4,1)S(1)}, s32[]{:S(2)}) async-start(s8[6291456]{0:T(1024)(128)(4,1)} %bitcast.588), calls=%async_computation.24 | async-start | bytes 4194304
  1027.9 278.7 %reduce-scatter.17.cloned.1.call-start = ((), (), s32[]{:S(2)}) async-start(), calls=%async_computation.16 | async-start | bytes 1966080 | tf_op jit(solution)/shard_map/reduce_scatter | solution.py:88
  1031.2 421.9 %all-reduce.6.cloned.1.call-start = ((), (), s32[]{:S(2)}) async-start(), calls=%async_computation.22 | async-start | bytes 18874368 | tf_op jit(solution)/shard_map/psum | solution.py:451
  1044.1 165.5 %copy-start.38 = (bf16[768,512]{1,0:T(8,128)(2,1)S(1)}, bf16[768,512]{1,0:T(8,128)(2,1)}, u32[]{:S(2)}) copy-start(bf16[768,512]{1,0:T(8,128)(2,1)} %copy-done.36) | copy-start | bytes 2359300
  1293.8 55.5 %copy-start.115 = (f32[768]{0:T(1024)S(1)}, f32[768]{0:T(1024)}, u32[]{:S(2)}) copy-start(f32[768]{0:T(1024)} %param.37) | copy-start | bytes 9220
  1293.8 56.8 %copy-start.116 = (f32[768]{0:T(1024)S(1)}, f32[768]{0:T(1024)}, u32[]{:S(2)}) copy-start(f32[768]{0:T(1024)} %param.38) | copy-start | bytes 9220
  1293.8 58.1 %copy-start.89 = (f32[768,16]{0,1:T(8,128)S(1)}, f32[768,16]{0,1:T(8,128)}, u32[]{:S(2)}) copy-start(f32[768,16]{0,1:T(8,128)} %param.39) | copy-start | bytes 147460
  1303.1 52.0 %copy-start.76 = (f32[768,16]{0,1:T(8,128)S(1)}, f32[768,16]{0,1:T(8,128)}, u32[]{:S(2)}) copy-start(f32[768,16]{0,1:T(8,128)} %param.30) | copy-start | bytes 147460
  1303.1 52.6 %copy-start.52 = (f32[128,768]{1,0:T(8,128)S(1)}, f32[128,768]{1,0:T(8,128)}, u32[]{:S(2)}) copy-start(f32[128,768]{1,0:T(8,128)} %get-tuple-element.300) | copy-start | bytes 1179652
  1303.1 52.6 %copy-start.119 = (f32[128]{0:T(128)S(1)}, f32[128]{0:T(128)}, u32[]{:S(2)}) copy-start(f32[128]{0:T(128)} %get-tuple-element.342) | copy-start | bytes 1540
  1303.1 55.4 %copy-start.60 = (f32[96,3,192]{0,2,1:T(8,128)S(1)}, f32[96,3,192]{0,2,1:T(8,128)}, u32[]{:S(2)}) copy-start(f32[96,3,192]{0,2,1:T(8,128)} %get-tuple-element.292) | copy-start | bytes 663556
  1349.2 115.8 %copy-start.90 = (f32[768,16]{0,1:T(8,128)}, f32[768,16]{0,1:T(8,128)S(1)}, u32[]{:S(2)}) copy-start(f32[768,16]{0,1:T(8,128)S(1)} %get-tuple-element.284) | copy-start | bytes 147460
  1349.2 115.8 %copy-start.117 = (f32[768]{0:T(1024)}, f32[768]{0:T(1024)S(1)}, u32[]{:S(2)}) copy-start(f32[768]{0:T(1024)S(1)} %get-tuple-element.282) | copy-start | bytes 9220
  1349.2 115.8 %copy-start.118 = (f32[768]{0:T(1024)}, f32[768]{0:T(1024)S(1)}, u32[]{:S(2)}) copy-start(f32[768]{0:T(1024)S(1)} %get-tuple-element.283) | copy-start | bytes 9220
  1349.8 115.1 %copy-start.104 = (f32[768]{0:T(1024)}, f32[768]{0:T(1024)S(1)}, u32[]{:S(2)}) copy-start(f32[768]{0:T(1024)S(1)} %get-tuple-element.298) | copy-start | bytes 9220
  1351.1 113.8 %copy-start.105 = (f32[768]{0:T(1024)}, f32[768]{0:T(1024)S(1)}, u32[]{:S(2)}) copy-start(f32[768]{0:T(1024)S(1)} %get-tuple-element.296) | copy-start | bytes 9220
  1352.5 112.5 %copy-start.83 = (f32[768,16]{0,1:T(8,128)}, f32[768,16]{0,1:T(8,128)S(1)}, u32[]{:S(2)}) copy-start(f32[768,16]{0,1:T(8,128)S(1)} %get-tuple-element.294) | copy-start | bytes 147460
  1359.3 105.7 %copy-start.122 = (bf16[768,512]{1,0:T(8,128)(2,1)S(1)}, bf16[768,512]{1,0:T(8,128)(2,1)}, u32[]{:S(2)}) copy-start(bf16[768,512]{1,0:T(8,128)(2,1)} %add_convert_fusion.4) | copy-start | bytes 2359300
  (95 other events, 488.7 us)
Sparse Core Ops, SparseCore 0:
  103.8 26.1 reduce-scatter.10
  431.7 27.5 reduce-scatter.12
  1028.0 169.1 all-reduce.3
  1200.2 28.3 reduce-scatter.16
  1281.8 171.2 all-reduce.5
Sparse Core Ops, SparseCore 1:
  279.5 76.6 all-gather.2
  498.7 119.2 reduce-scatter.20
  623.7 102.0 reduce-scatter.22
  729.4 26.4 reduce-scatter.14
  758.1 54.7 all-gather.4
  816.8 62.4 reduce-scatter.18
  883.6 66.8 reduce-scatter.24
where the time goes:
time: 1580 us; the launch traced here: 1560 us
  waiting for transfers between devices  542 us (34%)
  blocking collectives  389 us (25%)
  matrix products  219 us (14%)
  local copies, waits for them, and re-layouts  202 us (13%)
  other arithmetic  166 us (11%)
  between operations  27.8 us (2%)
  starting transfers between devices  19.8 us (1%)
    psum x2, waiting for transfers between devices, local(): lax.psum(jnp.stack([gram_term(matrix).astype(jnp.bfloat16).astype(jnp.flo...  247 us
    all_to_all x2, waiting for transfers between devices, send_owner(): return lax.all_to_all(values, 'dp', split_axis=0, concat_axis=0, tiled=True)  149 us
    all_gather x1, blocking collectives, local(): lax.all_gather(dense_out.astype(jnp.bfloat16), 'dp', axis=0, tiled=True)  112 us
    dot_general x16, matrix products, local(): jnp.dot(polynomial, matrix, preferred_element_type=jnp.float32)  103 us
    all_to_all x2, waiting for transfers between devices, send_source(): return lax.all_to_all(values, 'dp', split_axis=0, concat_axis=0, tiled=True)  62.3 us
    psum x1, blocking collectives, local(): lax.psum((grad_router, grad_first, grad_second, loss_local), ('dp', 'mp'))  41.4 us
    all_gather x1, blocking collectives, local(): lax.all_gather(attention_in.astype(jnp.bfloat16), 'dp', axis=0, tiled=True)  39.1 us
    dot_general x16, matrix products, gram_term(): jnp.einsum('dc,ec->de', matrix, matrix, preferred_element_type=jnp.float32)  38.6 us
  transfers between devices with their start and end apart: 16, of which 8 were waited for; matrix products, arithmetic and copies ran while one was open for 21% of the time, Pallas kernels for 0%

commit v1 on v0

v1 whole, which is shorter than its diff:
```python
import jax
import jax.numpy as jnp
from jax import lax
from jax.sharding import Mesh
from jax.sharding import PartitionSpec as P

D = 768
HEADS = 12
HEAD_DIM = 64
FF = 2048

highest = lax.Precision.HIGHEST
bf16 = jnp.bfloat16
f32 = jnp.float32
norm_eps = 1e-06
rope_base = 10000.0
masked_score = -1e30
ns_first = 3.4445
ns_second = -4.775
ns_third = 2.0315
decay_rate = 0.5
gain_rate = 0.05
router_rate = 0.02

DP = ("z", "y")
MP = ("x", "c")
SPARE = 64


def rms_scale(values):
    return lax.rsqrt(jnp.mean(values * values, axis=-1, keepdims=True) + norm_eps)


def rotate(values, cosine, sine_part):
    half_dim = values.shape[-1] // 2
    first_half = values[..., :half_dim]
    second = values[..., half_dim:]
    return jnp.concatenate(
        [first_half * cosine - second * sine_part, second * cosine + first_half * sine_part],
        axis=-1,
    )


def swiglu_back(gate_values, up_values, grad_inner):
    sigmoid_gate = jax.nn.sigmoid(gate_values)
    grad_gate_part = (
        grad_inner * up_values * sigmoid_gate * (1.0 + gate_values * (1.0 - sigmoid_gate))
    )
    grad_up_part = grad_inner * gate_values * sigmoid_gate
    return grad_gate_part.astype(bf16), grad_up_part.astype(bf16)


def norm_back(grad_normed, inputs, row_scale, norm_gain):
    scaled = grad_normed * norm_gain
    return row_scale * scaled - inputs * row_scale**3 * jnp.mean(
        scaled * inputs, axis=-1, keepdims=True
    )


def mm(left, right):
    return jnp.dot(left, right, preferred_element_type=f32)


def mm_t(left, right):
    return lax.dot_general(left, right, (((1,), (1,)), ((), ())), preferred_element_type=f32)


def t_mm(left, right):
    return lax.dot_general(left, right, (((0,), (0,)), ((), ())), preferred_element_type=f32)


def gather_rows(values):
    return lax.all_gather(values, MP, axis=0, tiled=True)


def scatter_rows(values):
    parts = lax.all_to_all(values.astype(bf16), MP, split_axis=0, concat_axis=0, tiled=True)
    return jnp.sum(parts.reshape(lax.axis_size(MP), -1, values.shape[1]).astype(f32), axis=0)


def gather_shards(values):
    paired = lax.all_gather(values, "y", axis=0, tiled=True)
    return lax.all_gather(paired, "z", axis=0, tiled=True)


def scatter_shards(values):
    parts = lax.all_to_all(values.astype(bf16), DP, split_axis=0, concat_axis=0, tiled=True)
    return jnp.sum(parts.reshape(lax.axis_size(DP), -1, values.shape[1]).astype(f32), axis=0)


def exchange(values):
    return lax.all_to_all(values, DP, split_axis=0, concat_axis=0, tiled=True)


def gram_term(matrix):
    return mm_t(matrix, matrix).astype(bf16)


def bmm(left, right):
    return jnp.einsum("nij,njk->nik", left, right, preferred_element_type=f32)


def step_matrices(grams):
    inverse = 1.0 / (jnp.trace(grams, axis1=1, axis2=2) + 1e-12)
    first_gram = grams * inverse[:, None, None]
    first_low = first_gram.astype(bf16)
    first_poly = (ns_second * first_gram + ns_third * bmm(first_low, first_low)).astype(bf16)
    mixed = bmm(first_poly, first_low)
    second_gram = (
        ns_first * ns_first * first_gram
        + 2.0 * ns_first * mixed
        + bmm(mixed.astype(bf16), first_poly)
    )
    second_low = second_gram.astype(bf16)
    second_poly = (ns_second * second_gram + ns_third * bmm(second_low, second_low)).astype(bf16)
    combined = ns_first * (first_poly.astype(f32) + second_poly.astype(f32)) + bmm(
        second_poly, first_poly
    )
    return combined.astype(bf16), inverse


def normed_delta(moment, step_rate):
    return -step_rate * moment * lax.rsqrt(jnp.mean(moment * moment) + 1e-12)


def local(
    tokens,
    teacher,
    segments,
    valid_mask,
    routes,
    first_gain,
    second_gain,
    router_weight,
    attention_in,
    attention_out,
    dense_in,
    dense_out,
    expert_in,
    expert_out,
    moment_first_gain,
    moment_second_gain,
    moment_router,
    moment_attention_in,
    moment_attention_out,
    moment_dense_in,
    moment_dense_out,
    moment_expert_in,
    moment_expert_out,
):
    row_count, width = tokens.shape
    mp_ways = lax.axis_size(MP)
    dp_ways = lax.axis_size(DP)
    mp_place = lax.axis_index(MP)
    dp_place = lax.axis_index(DP)
    core_place = lax.axis_index("c")
    seq_len = row_count * mp_ways
    expert_total = router_weight.shape[1]
    capacity = 4 * seq_len // expert_total
    half_cap = capacity // 2
    shard_rows = attention_in.shape[0]
    slabs = expert_in.shape[0]
    units = expert_in.shape[3]
    dense_units = dense_in.shape[2]
    sharing = FF // (units * mp_ways)
    heads_here = attention_in.shape[2] // HEAD_DIM
    head_cols = attention_in.shape[2]
    project_cols = 3 * head_cols
    project_scale = (3 * HEADS * HEAD_DIM / D) ** 0.5
    mix_scale = (HEADS * HEAD_DIM / D) ** 0.5
    pair_scale = (2 * FF / D) ** 0.5
    single_scale = (FF / D) ** 0.5
    slab_pair_scale = (2 * FF / (sharing * D)) ** 0.5
    slab_single_scale = (FF / (sharing * D)) ** 0.5

    mask_float = valid_mask.astype(f32)
    own_count = jnp.sum(mask_float)
    high_count = jnp.floor(own_count / 256.0)
    count_cells = jnp.zeros((shard_rows, SPARE), f32)
    count_cells = count_cells.at[0, 0].set(high_count)
    count_cells = count_cells.at[1, 0].set(own_count - 256.0 * high_count)
    first_pack = jnp.concatenate(
        [attention_in.reshape(shard_rows, project_cols), count_cells], axis=1
    ).astype(bf16)
    first_full = gather_shards(first_pack)
    weight_project = first_full[:, :project_cols]
    counts = first_full[:, project_cols].astype(f32).reshape(dp_ways, shard_rows)
    valid_count = jnp.sum(256.0 * counts[:, 0] + counts[:, 1])
    weight_mix = gather_shards(attention_out.astype(bf16))
    second_pack = jnp.concatenate(
        [dense_in[:, 0, :], dense_in[:, 1, :], dense_out], axis=1
    ).astype(bf16)
    second_full = lax.all_gather(second_pack, DP, axis=0, tiled=True)
    weight_pair = second_full[:, : 2 * dense_units]
    weight_down = second_full[:, 2 * dense_units :]
    router_low = router_weight.astype(bf16)
    expert_gate = expert_in[:, :, 0, :].astype(bf16)
    expert_up = expert_in[:, :, 1, :].astype(bf16)
    expert_down = expert_out.astype(bf16)

    onehot = (
        routes[:, :, None] == jnp.arange(expert_total, dtype=jnp.int32)[None, None, :]
    ).astype(f32)
    order = jnp.arange(seq_len, dtype=jnp.int32)
    earlier = mm(
        (order[:, None] > order[None, :]).astype(bf16), jnp.sum(onehot, axis=1).astype(bf16)
    )
    ranks = jnp.sum(onehot * earlier[:, None, :], axis=-1).astype(jnp.int32)
    half_ranks = ranks - core_place * half_cap
    here = (half_ranks >= 0) & (half_ranks < half_cap)
    slot_ids = jnp.where(here, routes * half_cap + half_ranks, -1)
    slot_total = expert_total * half_cap
    slot_order = jnp.arange(slot_total, dtype=jnp.int32)
    picks = [(slot_ids[:, k][:, None] == slot_order[None, :]) for k in range(2)]
    select = (picks[0] | picks[1]).astype(bf16)

    token_float = tokens.astype(f32)
    scale_one = rms_scale(token_float)
    full_one = gather_rows((token_float * scale_one * first_gain).astype(bf16))
    projected = mm(full_one, weight_project).reshape(seq_len, 3, heads_here, HEAD_DIM)
    positions = jnp.arange(seq_len, dtype=f32)
    frequency = rope_base ** (-jnp.arange(HEAD_DIM // 2, dtype=f32) * 2.0 / HEAD_DIM)
    angles = positions[:, None] * frequency[None, :]
    cosine = jnp.cos(angles)[:, None, :]
    sine = jnp.sin(angles)[:, None, :]
    query_scale = HEAD_DIM ** (-0.5)
    queries = (rotate(projected[:, 0], cosine, sine) * query_scale).astype(bf16)
    key_rows = rotate(projected[:, 1], cosine, sine).astype(bf16)
    value_rows = projected[:, 2].astype(bf16)
    allowed = (segments[:, None] == segments[None, :]) & (order[:, None] >= order[None, :])

    def head_scores():
        scores = jnp.einsum("qhd,khd->hqk", queries, key_rows, preferred_element_type=f32)
        return jnp.where(allowed[None], scores, masked_score)

    scores = head_scores()
    row_peak = jnp.max(scores, axis=-1, keepdims=True)
    exponent = jnp.exp(scores - row_peak)
    row_total = jnp.sum(exponent, axis=-1, keepdims=True)
    probs = exponent / row_total
    probs_low = probs.astype(bf16)
    mixed_low = (
        jnp.einsum("hqk,khd->qhd", probs_low, value_rows, preferred_element_type=f32)
        .astype(bf16)
        .reshape(seq_len, head_cols)
    )
    log_totals = row_peak + jnp.log(row_total)
    attended = scatter_rows(mm_t(mixed_low, weight_mix))
    hidden = token_float + attended
    scale_two = rms_scale(hidden)
    full_two = gather_rows((hidden * scale_two * second_gain).astype(bf16))

    dispatched = t_mm(select, full_two).astype(bf16)

    def to_owners(rows):
        spread = jnp.broadcast_to(
            rows.reshape(expert_total, 1, half_cap, width),
            (expert_total, sharing, half_cap, width),
        ).reshape(expert_total * sharing, half_cap, width)
        moved = exchange(spread).reshape(dp_ways, slabs, half_cap, width)
        both = lax.all_gather(moved, "c", axis=0)
        return [both[:, :, slab].reshape(-1, width) for slab in range(slabs)]

    def to_sources(parts):
        stacked = jnp.stack(
            [part.reshape(2, dp_ways, half_cap, width) for part in parts], axis=2
        )
        swapped = lax.all_to_all(stacked, "c", split_axis=0, concat_axis=0, tiled=True)
        halves = (swapped[0].astype(f32) + swapped[1].astype(f32)).astype(bf16)
        moved = exchange(halves.reshape(dp_ways * slabs, half_cap, width))
        moved = moved.reshape(expert_total, sharing, half_cap, width)
        if sharing > 1:
            moved = jnp.sum(moved.astype(f32), axis=1).astype(bf16)
        return moved.reshape(slot_total, width)

    received = to_owners(dispatched)

    gate_up = mm(full_two, weight_pair)
    gate_part = gate_up[:, :dense_units]
    up_part = gate_up[:, dense_units:]
    dense_inner = (jax.nn.silu(gate_part) * up_part).astype(bf16)
    dense_part = mm_t(dense_inner, weight_down)
    logits = mm(full_two, router_low)
    chosen = jnp.sum(onehot * logits[:, None, :], axis=-1)
    gate_probs = jax.nn.softmax(chosen, axis=-1)
    weighted = (
        jnp.where(picks[0], gate_probs[:, 0:1], 0.0) + jnp.where(picks[1], gate_probs[:, 1:2], 0.0)
    ).astype(bf16)

    slab_gate, slab_up, slab_inner, slab_parts = [], [], [], []
    for slab in range(slabs):
        gate_values = mm(received[slab], expert_gate[slab])
        up_values = mm(received[slab], expert_up[slab])
        inner = (jax.nn.silu(gate_values) * up_values).astype(bf16)
        slab_gate.append(gate_values)
        slab_up.append(up_values)
        slab_inner.append(inner)
        slab_parts.append(mm_t(inner, expert_down[slab]).astype(bf16))
    expert_rows = to_sources(slab_parts)
    branch = scatter_rows(dense_part + mm(weighted, expert_rows))
    output = hidden + branch
    errors = output - teacher.astype(f32)
    own_mask = lax.dynamic_slice_in_dim(mask_float, mp_place * row_count, row_count, 0)
    loss_local = jnp.sum(jnp.sum(errors * errors, axis=-1) * own_mask)
    factor = seq_len * dp_ways / valid_count
    grad_output = errors * (own_mask * factor)[:, None]
    grad_branch = gather_rows(grad_output.astype(bf16))

    raw_slots = t_mm(select, grad_branch)
    slot_gates = jnp.sum(
        jnp.where(picks[0], gate_probs[:, 0:1], 0.0) + jnp.where(picks[1], gate_probs[:, 1:2], 0.0),
        axis=0,
    )
    grad_slots = (raw_slots * slot_gates[:, None]).astype(bf16)
    grad_received = to_owners(grad_slots)
    slot_dots = jnp.sum(raw_slots * expert_rows.astype(f32), axis=-1)
    grad_chosen_raw = jnp.stack(
        [jnp.sum(jnp.where(pick, slot_dots[None, :], 0.0), axis=-1) for pick in picks], axis=-1
    )
    grad_chosen = gate_probs * (
        grad_chosen_raw - jnp.sum(gate_probs * grad_chosen_raw, axis=-1, keepdims=True)
    )
    grad_logits = jnp.sum(onehot * grad_chosen[:, :, None], axis=1)
    logits_high = grad_logits.astype(bf16)
    logits_rest = (grad_logits - logits_high.astype(f32)).astype(bf16)
    grad_router = t_mm(full_two, logits_high) + t_mm(full_two, logits_rest)

    grad_dense_inner = mm(grad_branch, weight_down)
    grad_gate, grad_up = swiglu_back(gate_part, up_part, grad_dense_inner)
    grad_pair = jnp.concatenate([grad_gate, grad_up], axis=1)
    grad_down = t_mm(grad_branch, dense_inner)
    grad_dense_in = t_mm(full_two, grad_pair)
    grad_full_two = (
        mm_t(grad_pair, weight_pair) + mm_t(logits_high, router_low) + mm_t(logits_rest, router_low)
    )
    dense_shard = scatter_shards(jnp.concatenate([grad_dense_in, grad_down], axis=1))

    slab_dispatch, grad_expert_gate, grad_expert_up, grad_expert_down = [], [], [], []
    for slab in range(slabs):
        grad_inner = mm(grad_received[slab], expert_down[slab])
        grad_g, grad_u = swiglu_back(slab_gate[slab], slab_up[slab], grad_inner)
        slab_dispatch.append(
            (mm_t(grad_g, expert_gate[slab]) + mm_t(grad_u, expert_up[slab])).astype(bf16)
        )
        grad_expert_gate.append(t_mm(received[slab], grad_g))
        grad_expert_up.append(t_mm(received[slab], grad_u))
        grad_expert_down.append(t_mm(grad_received[slab], slab_inner[slab]))
    grad_slot_rows = to_sources(slab_dispatch)
    grad_normed_two = scatter_rows(grad_full_two + mm(select, grad_slot_rows))

    grad_expert_in = jnp.stack(
        [
            jnp.stack([grad_expert_gate[slab], grad_expert_up[slab]], axis=1)
            for slab in range(slabs)
        ]
    )
    grad_expert_out = jnp.stack(grad_expert_down)
    new_moment_expert_in = decay_rate * moment_expert_in + grad_expert_in
    new_moment_expert_out = decay_rate * moment_expert_out + grad_expert_out
    shard_pair = dense_shard[:, : 2 * dense_units].reshape(shard_rows, 2, dense_units)
    shard_down = dense_shard[:, 2 * dense_units :]
    new_moment_pair = decay_rate * moment_dense_in + shard_pair
    new_moment_down = decay_rate * moment_dense_out + shard_down
    dense_moments = lax.all_gather(
        jnp.concatenate(
            [new_moment_pair[:, 0, :], new_moment_pair[:, 1, :], new_moment_down], axis=1
        ).astype(bf16),
        DP,
        axis=0,
        tiled=True,
    )
    full_pair = dense_moments[:, : 2 * dense_units]
    full_down = dense_moments[:, 2 * dense_units :]
    early = [full_pair, full_down]
    for slab in range(slabs):
        early.append(
            jnp.concatenate(
                [new_moment_expert_in[slab, :, 0, :], new_moment_expert_in[slab, :, 1, :]], axis=1
            ).astype(bf16)
        )
        early.append(new_moment_expert_out[slab].astype(bf16))
    early_grams = lax.psum(jnp.stack([gram_term(matrix) for matrix in early]), MP)
    share = len(early) // 2
    own_grams = lax.dynamic_slice_in_dim(early_grams, core_place * share, share, 0).astype(f32)
    own_steps, own_inverse = step_matrices(own_grams)
    early_steps = lax.all_gather(own_steps, "c", axis=0, tiled=True)
    early_inverse = lax.all_gather(own_inverse, "c", axis=0, tiled=True)

    grad_hidden = norm_back(grad_normed_two, hidden, scale_two, second_gain) + grad_output
    grad_second_part = jnp.sum(grad_normed_two * hidden * scale_two, axis=0)
    grad_attended = gather_rows(grad_hidden.astype(bf16))
    grad_mix = t_mm(grad_attended, mixed_low)
    grad_mixed = (
        mm(grad_attended, weight_mix).astype(bf16).reshape(seq_len, heads_here, HEAD_DIM)
    )
    score_weights = jnp.exp(head_scores() - log_totals)
    grad_weights = jnp.einsum("qhd,khd->hqk", grad_mixed, value_rows, preferred_element_type=f32)
    row_dots = jnp.sum(grad_weights * score_weights, axis=-1, keepdims=True)
    grad_scores = (score_weights * (grad_weights - row_dots)).astype(bf16)
    grad_queries = jnp.einsum("hqk,khd->qhd", grad_scores, key_rows, preferred_element_type=f32)
    grad_keys = jnp.einsum("hqk,qhd->khd", grad_scores, queries, preferred_element_type=f32)
    grad_values = jnp.einsum(
        "hqk,qhd->khd", score_weights.astype(bf16), grad_mixed, preferred_element_type=f32
    )
    grad_projected = jnp.concatenate(
        [
            rotate(grad_queries * query_scale, cosine, -sine).reshape(seq_len, head_cols),
            rotate(grad_keys, cosine, -sine).reshape(seq_len, head_cols),
            grad_values.reshape(seq_len, head_cols),
        ],
        axis=1,
    ).astype(bf16)
    grad_project = t_mm(full_one, grad_projected)
    grad_full_one = mm_t(grad_projected, weight_project)
    grad_first_part = jnp.sum(grad_full_one * full_one.astype(f32), axis=0) / first_gain

    loss_cells = jnp.zeros((width, 1), f32).at[0, 0].set(loss_local)
    small = jnp.concatenate(
        [grad_first_part[:, None], grad_second_part[:, None], grad_router, loss_cells], axis=1
    )
    small = jnp.pad(small, ((0, 0), (0, SPARE - small.shape[1])))
    mix_shard = scatter_shards(grad_mix)
    new_moment_mix = decay_rate * moment_attention_out + mix_shard
    last_shard = scatter_shards(jnp.concatenate([grad_project, small], axis=1))
    shard_project = last_shard[:, :project_cols].reshape(shard_rows, 3, head_cols)
    new_moment_project = decay_rate * moment_attention_in + shard_project
    last_moments = gather_shards(
        jnp.concatenate(
            [
                new_moment_project.reshape(shard_rows, project_cols),
                last_shard[:, project_cols:],
                new_moment_mix,
            ],
            axis=1,
        ).astype(bf16)
    )
    full_project = last_moments[:, :project_cols]
    full_mix = last_moments[:, project_cols + SPARE :]
    last_sums = lax.all_to_all(
        jnp.concatenate(
            [
                gram_term(full_project),
                gram_term(full_mix),
                last_moments[:, project_cols : project_cols + SPARE],
            ],
            axis=1,
        ),
        MP,
        split_axis=0,
        concat_axis=0,
        tiled=True,
    )
    last_sums = jnp.sum(last_sums.reshape(mp_ways, -1, last_sums.shape[1]).astype(f32), axis=0)
    last_sums = gather_rows(last_sums.astype(bf16))
    last_steps, last_inverse = step_matrices(
        jnp.stack([last_sums[:, :width], last_sums[:, width : 2 * width]]).astype(f32)
    )
    small_total = last_sums[:, 2 * width :].astype(f32)
    grad_normed_one = scatter_rows(grad_full_one)
    grad_tokens = norm_back(grad_normed_one, token_float, scale_one, first_gain) + grad_hidden

    first_total = small_total[:, 0]
    second_total = small_total[:, 1]
    router_total = small_total[:, 2 : 2 + expert_total]
    loss_total = small_total[0, 2 + expert_total]
    loss_value = loss_total / (valid_count * width)
    new_moment_first = decay_rate * moment_first_gain + first_total
    new_moment_second = decay_rate * moment_second_gain + second_total
    new_moment_router = decay_rate * moment_router + router_total

    def update(step, inverse, matrix, step_scale):
        full = ns_first * ns_first * matrix.astype(f32) + mm(step, matrix)
        return (-step_scale * jnp.sqrt(inverse)) * full

    def update_rows(step, inverse, matrix, step_scale):
        step_rows = lax.dynamic_slice_in_dim(step, dp_place * shard_rows, shard_rows, 0)
        own_rows = lax.dynamic_slice_in_dim(matrix, dp_place * shard_rows, shard_rows, 0)
        full = ns_first * ns_first * own_rows.astype(f32) + mm(step_rows, matrix)
        return (-step_scale * jnp.sqrt(inverse)) * full

    step_first = normed_delta(new_moment_first, gain_rate)
    step_second = normed_delta(new_moment_second, gain_rate)
    new_router = router_weight + normed_delta(new_moment_router, router_rate)
    new_attention_in = attention_in + update_rows(
        last_steps[0], last_inverse[0], full_project, project_scale
    ).reshape(attention_in.shape)
    step_mix = update_rows(last_steps[1], last_inverse[1], full_mix, mix_scale)
    new_dense_in = dense_in + update_rows(
        early_steps[0], early_inverse[0], full_pair, pair_scale
    ).reshape(dense_in.shape)
    new_dense_out = dense_out + update_rows(
        early_steps[1], early_inverse[1], full_down, single_scale
    )
    pair_steps, single_steps = [], []
    for slab in range(slabs):
        place = 2 + 2 * slab
        pair_steps.append(
            update(early_steps[place], early_inverse[place], early[place], slab_pair_scale).reshape(
                width, 2, units
            )
        )
        single_steps.append(
            update(
                early_steps[place + 1],
                early_inverse[place + 1],
                early[place + 1],
                slab_single_scale,
            )
        )
    new_expert_in = expert_in + jnp.stack(pair_steps)
    new_expert_out = expert_out + jnp.stack(single_steps)
    return (
        output.astype(bf16),
        loss_value,
        grad_tokens,
        first_total,
        second_total,
        router_total,
        shard_project,
        mix_shard,
        shard_pair,
        shard_down,
        grad_expert_in,
        grad_expert_out,
        new_moment_first,
        new_moment_second,
        new_moment_router,
        new_moment_project,
        new_moment_mix,
        new_moment_pair,
        new_moment_down,
        new_moment_expert_in,
        new_moment_expert_out,
        step_first,
        step_second,
        new_router,
        new_attention_in,
        step_mix,
        new_dense_in,
        new_dense_out,
        new_expert_in,
        new_expert_out,
    )


def solution(mesh):
    dp_ways, mp_ways = mesh.devices.shape
    fine_mesh = Mesh(
        mesh.devices.reshape(dp_ways // 2, 2, mp_ways // 2, 2), ("z", "y", "x", "c")
    )
    rows = P(("z", "y", "x", "c"), None)
    project = P(DP, None, MP)
    plain = P(DP, MP)
    slab_pair = P(DP, None, None, MP)
    slab_single = P(DP, None, MP)
    weights = (P(), P(), P(), project, plain, project, plain, slab_pair, slab_single)
    return jax.shard_map(
        local,
        mesh=fine_mesh,
        in_specs=(rows, rows, P(DP), P(DP), P(DP, None)) + weights + weights,
        out_specs=(rows, P(), rows) + weights + weights + weights,
        check_vma=False,
    )
```

time: 1580 us -> 947 us (0.60)
  waiting for transfers between devices: 542 us -> 267 us
  blocking collectives: 389 us -> 188 us
  local copies, waits for them, and re-layouts: 202 us -> 114 us
  other arithmetic: 166 us -> 97.9 us
  starting transfers between devices: 19.8 us -> 43.9 us
  matrix products: 219 us -> 197 us
    all_gather x10 -> x9, blocking collectives: 321 us -> 88.9 us  [the longest x2 37 us: gather_shards(): return lax.all_gather(paired, 'z', axis=0, tiled=True)]
    psum x2 -> x1, waiting for transfers between devices: 247 us -> 114 us  [local(): lax.psum(jnp.stack([gram_term(matrix) for matrix in early]), MP)]
    all_to_all x4 -> x10, waiting for transfers between devices: 211 us -> 85.9 us  [the longest x3 41.6 us: scatter_shards(): lax.all_to_all(values.astype(bf16), DP, split_axis=0, concat_axis=0, tile...]
    all_to_all x0 -> x4, blocking collectives: none -> 96.8 us  [the longest x2 83.3 us: exchange(): return lax.all_to_all(values, DP, split_axis=0, concat_axis=0, tiled=True)]
    psum x3 -> x0, blocking collectives: 67.6 us -> none  [the longest x1 41.4 us: local(): lax.psum((grad_router, grad_first, grad_second, loss_local), ('dp', 'mp'))]
    all_gather x2 -> x7, waiting for transfers between devices: 0.01 us -> 66.7 us  [the longest x1 50.9 us: local(): second_full = lax.all_gather(second_pack, DP, axis=0, tiled=True)]
    gather x8 -> x0, local copies, waits for them, and re-layouts: 57.6 us -> none  [the longest x2 15.4 us: local(): picked = expert_rows[slot_ids].reshape(seq_len, 2, model_width)]
    reduce_scatter x7 -> x0, waiting for transfers between devices: 47.7 us -> none  [the longest x1 26.8 us: local(): lax.psum_scatter(grad_mix, 'dp', scatter_dimension=0, tiled=True)]
  transfers between devices with their start and end apart: 16 -> 18, of which waited for: 8 -> 11; matrix products, arithmetic and copies ran while one was open for 21% -> 32% of each run, Pallas kernels for 0% -> 0%
where the time goes in v1:
time: 947 us; the launch traced here: 937 us
  waiting for transfers between devices  267 us (28%)
  matrix products  197 us (21%)
  blocking collectives  188 us (20%)
  local copies, waits for them, and re-layouts  114 us (12%)
  other arithmetic  97.9 us (10%)
  starting transfers between devices  43.9 us (5%)
  between operations  29.2 us (3%)
    psum x1, waiting for transfers between devices, local(): lax.psum(jnp.stack([gram_term(matrix) for matrix in early]), MP)  114 us
    all_to_all x2, blocking collectives, exchange(): return lax.all_to_all(values, DP, split_axis=0, concat_axis=0, tiled=True)  83.3 us
    dot_general x10, matrix products, bmm(): return jnp.einsum('nij,njk->nik', left, right, preferred_element_type=f32)  77.3 us
    unnamed x299, local copies, waits for them, and re-layouts  70.5 us
    all_gather x1, waiting for transfers between devices, local(): second_full = lax.all_gather(second_pack, DP, axis=0, tiled=True)  50.9 us
    dot_general x22, matrix products, mm(): return jnp.dot(left, right, preferred_element_type=f32)  42 us
    all_to_all x3, waiting for transfers between devices, scatter_shards(): lax.all_to_all(values.astype(bf16), DP, split_axis=0, concat_axis=0, tile...  41.6 us
    dot_general x20, matrix products, mm_t(): lax.dot_general(left, right, (((1,), (1,)), ((), ())), preferred_element_...  39.6 us
  transfers between devices with their start and end apart: 18, of which 11 were waited for; matrix products, arithmetic and copies ran while one was open for 32% of the time, Pallas kernels for 0%

profile of v1, /device:TPU:0, one launch (start us, length us, event | category | flops | bytes accessed | tf_op | source)
XLA Modules:
  0.0 936.9 jit_solution(3763960560452778896)
XLA Ops:
  12.4 5.7 all_gather.54
  19.5 5.6 all_gather.52
  26.3 15.9 %all_gather.55 = bf16[768,192]{1,0:T(8,128)(2,1)S(1)} all-gather(bf16[192,192]{1,0:T(8,128)(2,1)S(1)} %all_gather.54), channel_id=1, replica_groups=mesh['z'=4,'y'=2,'x'=2,'c'=2] {'z'}, dimensions={0}, use_global_device_ids=true | all-gather | bytes 368640 | tf_op jit(solution)/shard_map/all_gather | solution.py:83
  42.2 8.6 all_gather.51
  50.8 21.1 %all_gather.53 = bf16[768,640]{1,0:T(8,128)(2,1)S(1)} all-gather(bf16[192,640]{1,0:T(8,128)(2,1)S(1)} %all_gather.52), channel_id=1, replica_groups=mesh['z'=4,'y'=2,'x'=2,'c'=2] {'z'}, dimensions={0}, use_global_device_ids=true | all-gather | bytes 1228800 | tf_op jit(solution)/shard_map/all_gather | solution.py:83
  78.0 4.3 all-to-all-start
  83.2 10.8 %all-to-all-done = bf16[4,128,768]{2,1,0:T(8,128)(2,1)} async-done(((bf16[4,128,768]{2,1,0:T(8,128)(2,1)}), bf16[4,128,768]{2,1,0:T(8,128)(2,1)}, u32[]{:S(2)}, u32[]{:S(2)}) %all-to-all-start) | async-done | bytes 786464 | tf_op jit(solution)/shard_map/all_to_all | solution.py:77
  97.1 8.0 all_gather.56
  107.5 42.4 %all_to_all.96 = bf16[16,64,768]{2,1,0:T(8,128)(2,1)} all-to-all(bf16[16,64,768]{2,1,0:T(8,128)(2,1)S(1)} %bitcast.315), channel_id=1, replica_groups=mesh['z'=4,'y'=2,'x'=2,'c'=2] {'z','y'}, dimensions={0} | all-to-all | bytes 3145728 | tf_op jit(solution)/shard_map/all_to_all | solution.py:92
  156.5 6.1 copy.392
  174.8 6.3 all_to_all.97
  182.7 4.3 all-to-all-start.3
  190.2 50.9 %all-gather.8.cloned.1.call-done = bf16[768,1536]{1,0:T(8,128)(2,1)} async-done(((bf16[96,1536]{1,0:T(8,128)(2,1)}), bf16[768,1536]{1,0:T(8,128)(2,1)}) %all-gather.8.cloned.1.call-update) | async-done | bytes 2359312 | tf_op jit(solution)/shard_map/all_gather | solution.py:193
  251.6 4.2 all-to-all-start.4
  270.6 8.4 all_gather.59
  284.4 40.9 %all_to_all.98 = bf16[16,64,768]{2,1,0:T(8,128)(2,1)} all-to-all(bf16[16,64,768]{2,1,0:T(8,128)(2,1)S(1)} %bitcast.300), channel_id=1, replica_groups=mesh['z'=4,'y'=2,'x'=2,'c'=2] {'z','y'}, dimensions={0} | all-to-all | bytes 3145728 | tf_op jit(solution)/shard_map/all_to_all | solution.py:92
  350.6 7.2 all_to_all.99
  357.8 6.0 all-to-all-start.13
  367.3 10.2 %copy.359 = f32[2,768,2,512]{1,3,2,0:T(8,128)} copy(f32[2,768,2,512]{3,2,1,0:T(2,128)} %param.50) | data formatting | bytes 12582912 | tf_op args[21]
  388.8 29.2 %all-to-all-done.13 = bf16[8,96,1536]{2,1,0:T(8,128)(2,1)} async-done(((bf16[8,96,1536]{2,1,0:T(8,128)(2,1)}), bf16[8,96,1536]{2,1,0:T(8,128)(2,1)}, u32[]{:S(2)}, u32[]{:S(2)}) %all-to-all-start.13) | async-done | bytes 2359328 | tf_op jit(solution)/shard_map/all_to_all | solution.py:87
  418.0 4.3 all-to-all-start.7
  444.3 24.2 %all-to-all-done.7 = bf16[16,64,768]{2,1,0:T(8,128)(2,1)} async-done(((bf16[16,64,768]{2,1,0:T(8,128)(2,1)}), bf16[16,64,768]{2,1,0:T(8,128)(2,1)}, u32[]{:S(2)}, u32[]{:S(2)}) %all-to-all-start.7) | async-done | bytes 1572896 | tf_op jit(solution)/shard_map/all_to_all | solution.py:92
  472.6 4.2 all-to-all-start.8
  483.2 5.4 all-to-all-done.8
  493.7 8.3 all_gather.61
  513.1 4.1 all-to-all-start.10
  529.7 4.3 all-to-all-start.9
  542.1 5.3 fusion.196
  549.9 8.3 all-to-all-done.9
  565.6 7.4 all_gather.62
  575.3 4.5 fusion.53
  593.9 11.9 %all-gather.14.cloned.1.call-done = bf16[768,832]{1,0:T(8,128)(2,1)} async-done(((bf16[192,832]{1,0:T(8,128)(2,1)}), bf16[768,832]{1,0:T(8,128)(2,1)}) %all-gather.14.cloned.1.call-update) | async-done | bytes 1277968 | tf_op jit(solution)/shard_map/all_gather | solution.py:83
  627.3 10.2 %copy.372 = f32[2,768,2,512]{3,2,1,0:T(2,128)} copy(f32[2,768,2,512]{1,3,2,0:T(8,128)} %get-tuple-element.289) | data formatting | bytes 12582912
  637.6 10.2 %copy.368 = f32[2,768,2,512]{3,2,1,0:T(2,128)} copy(f32[2,768,2,512]{1,3,2,0:T(8,128)} %get-tuple-element.314) | data formatting | bytes 12582912
  652.3 114.4 %all-reduce.6.cloned.1.call-done = bf16[6,768,768]{2,1,0:T(8,128)(2,1)} async-done(((bf16[6,768,768]{2,1,0:T(8,128)(2,1)}), bf16[6,768,768]{2,1,0:T(8,128)(2,1)}) %all-reduce.6.cloned.1.call-update) | async-done | bytes 7077904 | tf_op jit(solution)/shard_map/psum | solution.py:382
  771.9 7.5 fusion.4
  779.4 5.4 fusion.99
  787.8 5.0 fusion.21
  792.8 22.3 %add_convert_fusion.1 = bf16[3,768,768]{2,1,0:T(8,128)(2,1)} fusion(f32[3,768,768]{2,1,0:T(8,128)} %fusion.21, f32[3,768,768]{2,1,0:T(8,128)} %copy-done.5, f32[3]{0:T(128)S(1)} %get-tuple-element.287, bf16[6,768,768]{2,1,0:T(8,128)(2,1)} %all-reduce.6.cloned.1.call-done, s32[]{:T(128)S(6)} %select_n.60), kind=kOutput, calls=%fused_computation.11 | convolution fusion | flops 2747990016 | bytes 38930432 | tf_op jit(solution)/shard_map/nij,njk->nik/dot_general | solution.py:100
  815.1 8.0 add_convert_fusion
  854.3 4.2 fusion.32
  858.5 12.9 %add_convert_fusion.3 = bf16[2,768,768]{2,1,0:T(8,128)(2,1)} fusion(f32[2,768,768]{2,1,0:T(8,128)} %fusion.32, f32[2,768,768]{2,1,0:T(8,128)} %copy-done.18, f32[2]{0:T(128)S(1)} %add_divide_fusion.4, bf16[1,768,768]{2,1,0:T(8,128)(2,1)S(1)} %get-tuple-element.330, bf16[1,768,768]{2,1,0:T(8,128)(2,1)S(1)} %get-tuple-element.329), kind=kOutput, calls=%fused_computation.27 | convolution fusion | flops 1834352640 | bytes 14155784 | tf_op jit(solution)/shard_map/nij,njk->nik/dot_general | solution.py:100
  871.4 5.9 add_convert_fusion.2
  883.2 5.3 add_multiply_fusion
  888.5 4.2 copy.365
  892.7 5.3 add_multiply_fusion.1
  898.0 5.9 copy.364
  910.4 9.5 %maximum_add_fusion = f32[2,768,2,512]{3,2,1,0:T(2,128)} fusion(f32[2,768,2,512]{3,2,1,0:T(2,128)} %param.41, f32[1,768,2,512]{3,2,1,0:T(2,128)S(1)} %copy.365, f32[1,768,2,512]{3,2,1,0:T(2,128)} %copy.364), kind=kLoop, calls=%fused_computation.13 | loop fusion | flops 3145728 | bytes 18874368 | tf_op jit(solution)/shard_map/add | solution.py:510
  (517 shorter events, 283.2 us)
Async XLA Ops:
  7.2 34.9 %copy-start.12 = (bf16[128,768]{1,0:T(8,128)(2,1)S(1)}, bf16[128,768]{1,0:T(8,128)(2,1)}, u32[]{:S(2)}) copy-start(bf16[128,768]{1,0:T(8,128)(2,1)} %param.29) | copy-start | bytes 589828
  7.2 18.8 %copy-start.108 = (s32[512]{0:T(512)S(1)}, s32[512]{0:T(512)}, u32[]{:S(2)}) copy-start(s32[512]{0:T(512)} %param.31) | copy-start | bytes 6148
  7.2 34.9 %copy-start.95 = (f32[768]{0:T(1024)S(1)}, f32[768]{0:T(1024)}, u32[]{:S(2)}) copy-start(f32[768]{0:T(1024)} %param.34) | copy-start | bytes 9220
  11.5 60.5 %copy-start.122 = (f32[128]{0:T(128)}, f32[128]{0:T(128)S(1)}, u32[]{:S(2)}) copy-start(f32[128]{0:T(128)S(1)} %get-tuple-element.367) | copy-start | bytes 1540
  26.0 46.7 %copy-start.85 = (f32[512,32]{0,1:T(8,128)}, f32[512,32]{0,1:T(8,128)S(1)}, u32[]{:S(2)}) copy-start(f32[512,32]{0,1:T(8,128)S(1)} %get-tuple-element.370) | copy-start | bytes 196612
  26.2 48.8 %copy-start.6 = (pred[512,512]{0,1:T(8,128)(4,1)}, pred[512,512]{0,1:T(8,128)(4,1)S(1)}, u32[]{:S(2)}) copy-start(pred[512,512]{0,1:T(8,128)(4,1)S(1)} %fusion.97) | copy-start | bytes 786436
  42.1 34.5 %copy-start.21 = (bf16[768,192]{1,0:T(8,128)(2,1)}, bf16[768,192]{1,0:T(8,128)(2,1)S(1)}, u32[]{:S(2)}) copy-start(bf16[768,192]{1,0:T(8,128)(2,1)S(1)} %all_gather.55) | copy-start | bytes 884740
  50.8 21.8 %copy-start.29 = (bf16[512,768]{1,0:T(8,128)(2,1)}, bf16[512,768]{1,0:T(8,128)(2,1)S(1)}, u32[]{:S(2)}) copy-start(bf16[512,768]{1,0:T(8,128)(2,1)S(1)} %all_gather.51) | copy-start | bytes 2359300
  78.0 19.0 %copy-start.99 = (f32[768]{0:T(1024)S(1)}, f32[768]{0:T(1024)}, u32[]{:S(2)}) copy-start(f32[768]{0:T(1024)} %param.35) | copy-start | bytes 9220
  78.0 16.0 %all-to-all-start = ((bf16[4,128,768]{2,1,0:T(8,128)(2,1)}), bf16[4,128,768]{2,1,0:T(8,128)(2,1)}, u32[]{:S(2)}, u32[]{:S(2)}) async-start(bf16[4,128,768]{2,1,0:T(8,128)(2,1)} %bitcast.311), calls=%async_computation | async-start | bytes 1572864 | tf_op jit(solution)/shard_map/all_to_all | solution.py:77
  82.3 80.3 %all-gather.10.cloned.1.call-start = ((), (), s32[]{:S(2)}) async-start(), calls=%async_computation.15 | async-start | bytes 4718592 | tf_op jit(solution)/shard_map/all_gather | solution.py:261
  94.0 12.2 %copy-start.97 = (s32[512,2]{0,1:T(2,128)S(1)}, s32[512,2]{0,1:T(2,128)}, u32[]{:S(2)}) copy-start(s32[512,2]{0,1:T(2,128)} %param.33) | copy-start | bytes 12292
  94.0 12.2 %copy-start.102 = (f32[512,16]{0,1:T(8,128)S(1)}, f32[512,16]{0,1:T(8,128)}, u32[]{:S(2)}) copy-start(f32[512,16]{0,1:T(8,128)} %fusion.98) | copy-start | bytes 98308
  96.9 9.4 copy-start.118
  106.3 43.7 %copy-start.109 = (s32[512,1]{0,1:T(1,128)}, s32[512,1]{0,1:T(1,128)S(1)}, u32[]{:S(2)}) copy-start(s32[512,1]{0,1:T(1,128)S(1)} %get-tuple-element.356) | copy-start | bytes 6148
  106.3 43.7 %copy-start.112 = (s32[512,1]{0,1:T(1,128)}, s32[512,1]{0,1:T(1,128)S(1)}, u32[]{:S(2)}) copy-start(s32[512,1]{0,1:T(1,128)S(1)} %get-tuple-element.357) | copy-start | bytes 6148
  150.0 91.1 %all-gather.8.cloned.1.call-start = ((), (), s32[]{:S(2)}) async-start(), calls=%async_computation.14 | async-start | bytes 2654208 | tf_op jit(solution)/shard_map/all_gather | solution.py:193
  182.7 63.4 %all-to-all-start.3 = ((bf16[16,64,768]{2,1,0:T(8,128)(2,1)}), bf16[16,64,768]{2,1,0:T(8,128)(2,1)}, u32[]{:S(2)}, u32[]{:S(2)}) async-start(bf16[16,64,768]{2,1,0:T(8,128)(2,1)} %bitcast.299), calls=%async_computation.3 | async-start | bytes 3145728 | tf_op jit(solution)/shard_map/all_to_all | solution.py:92
  251.6 15.9 %all-to-all-start.4 = ((bf16[4,128,768]{2,1,0:T(8,128)(2,1)}), bf16[4,128,768]{2,1,0:T(8,128)(2,1)}, u32[]{:S(2)}, u32[]{:S(2)}) async-start(bf16[4,128,768]{2,1,0:T(8,128)(2,1)} %bitcast.308), calls=%async_computation.4 | async-start | bytes 1572864 | tf_op jit(solution)/shard_map/all_to_all | solution.py:77
  255.8 80.5 %all-gather.12.cloned.1.call-start = ((), (), s32[]{:S(2)}) async-start(), calls=%async_computation.16 | async-start | bytes 4718592 | tf_op jit(solution)/shard_map/all_gather | solution.py:261
  267.5 11.5 %copy-start.110 = (s32[512,1]{0,1:T(1,128)S(1)}, s32[512,1]{0,1:T(1,128)}, u32[]{:S(2)}) copy-start(s32[512,1]{0,1:T(1,128)} %copy-done.109) | copy-start | bytes 6148
  267.5 11.5 %copy-start.113 = (s32[512,1]{0,1:T(1,128)S(1)}, s32[512,1]{0,1:T(1,128)}, u32[]{:S(2)}) copy-start(s32[512,1]{0,1:T(1,128)} %copy-done.112) | copy-start | bytes 6148
  357.8 60.2 %all-to-all-start.13 = ((bf16[8,96,1536]{2,1,0:T(8,128)(2,1)}), bf16[8,96,1536]{2,1,0:T(8,128)(2,1)}, u32[]{:S(2)}, u32[]{:S(2)}) async-start(bf16[8,96,1536]{2,1,0:T(8,128)(2,1)} %pad_maximum_fusion.5), calls=%async_computation.13 | async-start | bytes 4718592 | tf_op jit(solution)/shard_map/all_to_all | solution.py:87
  418.0 50.5 %all-to-all-start.7 = ((bf16[16,64,768]{2,1,0:T(8,128)(2,1)}), bf16[16,64,768]{2,1,0:T(8,128)(2,1)}, u32[]{:S(2)}, u32[]{:S(2)}) async-start(bf16[16,64,768]{2,1,0:T(8,128)(2,1)} %bitcast.298), calls=%async_computation.7 | async-start | bytes 3145728 | tf_op jit(solution)/shard_map/all_to_all | solution.py:92
  422.3 152.9 %all-gather.18.cloned.1.call-start = ((), (), s32[]{:S(2)}) async-start(), calls=%async_computation.19 | async-start | bytes 2654208 | tf_op jit(solution)/shard_map/all_gather | solution.py:364
  442.1 26.4 %copy-start.111 = (s32[512,1]{0,1:T(1,128)S(1)}, s32[512,1]{0,1:T(1,128)}, u32[]{:S(2)}) copy-start(s32[512,1]{0,1:T(1,128)} %copy-done.109) | copy-start | bytes 6148
  442.1 26.4 %copy-start.114 = (s32[512,1]{0,1:T(1,128)S(1)}, s32[512,1]{0,1:T(1,128)}, u32[]{:S(2)}) copy-start(s32[512,1]{0,1:T(1,128)} %copy-done.112) | copy-start | bytes 6148
  472.6 15.9 %all-to-all-start.8 = ((bf16[4,128,768]{2,1,0:T(8,128)(2,1)}), bf16[4,128,768]{2,1,0:T(8,128)(2,1)}, u32[]{:S(2)}, u32[]{:S(2)}) async-start(bf16[4,128,768]{2,1,0:T(8,128)(2,1)} %bitcast.312), calls=%async_computation.8 | async-start | bytes 1572864 | tf_op jit(solution)/shard_map/all_to_all | solution.py:77
  483.1 9.6 %copy-start.117 = (f32[128]{0:T(128)S(1)}, f32[128]{0:T(128)}, u32[]{:S(2)}) copy-start(f32[128]{0:T(128)} %broadcast_multiply_fusion.2) | copy-start | bytes 1540
  489.9 12.1 %copy-start.22 = (bf16[768,192]{1,0:T(8,128)(2,1)S(1)}, bf16[768,192]{1,0:T(8,128)(2,1)}, u32[]{:S(2)}) copy-start(bf16[768,192]{1,0:T(8,128)(2,1)} %copy-done.21) | copy-start | bytes 884740
  491.3 11.2 %copy-start.83 = (bf16[3,64,512]{2,1,0:T(8,128)(2,1)S(1)}, bf16[3,64,512]{2,1,0:T(8,128)(2,1)}, u32[]{:S(2)}) copy-start(bf16[3,64,512]{2,1,0:T(8,128)(2,1)} %copy-done.82) | copy-start | bytes 589828
  493.7 9.8 %copy-start.7 = (pred[512,512]{0,1:T(8,128)(4,1)S(1)}, pred[512,512]{0,1:T(8,128)(4,1)}, u32[]{:S(2)}) copy-start(pred[512,512]{0,1:T(8,128)(4,1)} %copy-done.6) | copy-start | bytes 786436
  493.7 9.8 %copy-start.94 = (f32[3,512]{1,0:T(4,128)S(1)}, f32[3,512]{1,0:T(4,128)}, u32[]{:S(2)}) copy-start(f32[3,512]{1,0:T(4,128)} %log_add_fusion) | copy-start | bytes 18436
  508.0 9.2 copy-start.86
  508.0 9.2 copy-start.90
  513.1 16.6 %all-to-all-start.10 = ((bf16[8,96,192]{1,2,0:T(8,128)(2,1)}), bf16[8,96,192]{1,2,0:T(8,128)(2,1)}, u32[]{:S(2)}, u32[]{:S(2)}) async-start(bf16[8,96,192]{1,2,0:T(8,128)(2,1)} %copy.351), calls=%async_computation.10 | async-start | bytes 786432 | tf_op jit(solution)/shard_map/all_to_all | solution.py:87
  529.7 28.5 %all-to-all-start.9 = ((bf16[8,96,640]{2,1,0:T(8,128)(2,1)}), bf16[8,96,640]{2,1,0:T(8,128)(2,1)}, u32[]{:S(2)}, u32[]{:S(2)}) async-start(bf16[8,96,640]{2,1,0:T(8,128)(2,1)} %pad_maximum_fusion.14), calls=%async_computation.9 | async-start | bytes 1966080 | tf_op jit(solution)/shard_map/all_to_all | solution.py:87
  534.0 71.8 %all-gather.14.cloned.1.call-start = ((), (), s32[]{:S(2)}) async-start(), calls=%async_computation.17 | async-start | bytes 1720320 | tf_op jit(solution)/shard_map/all_gather | solution.py:83
  561.4 13.9 %copy-start.31 = (f32[96,576]{0,1:T(8,128)}, f32[96,576]{0,1:T(8,128)S(1)}, u32[]{:S(2)}) copy-start(f32[96,576]{0,1:T(8,128)S(1)} %copy.349) | copy-start | bytes 663556
  573.1 193.7 %all-reduce.6.cloned.1.call-start = ((), (), s32[]{:S(2)}) async-start(), calls=%async_computation.20 | async-start | bytes 14155776 | tf_op jit(solution)/shard_map/psum | solution.py:382
  590.4 26.1 %all-to-all-start.12 = ((bf16[4,128,768]{2,1,0:T(8,128)(2,1)}), bf16[4,128,768]{2,1,0:T(8,128)(2,1)S(1)}, u32[]{:S(2)}, u32[]{:S(2)}) async-start(bf16[4,128,768]{2,1,0:T(8,128)(2,1)} %bitcast.61), calls=%async_computation.12 | async-start | bytes 1572864 | tf_op jit(solution)/shard_map/all_to_all | solution.py:77
  617.4 153.1 %all-to-all-start.11 = ((bf16[4,192,1600]{2,1,0:T(8,128)(2,1)}), bf16[4,192,1600]{2,1,0:T(8,128)(2,1)S(1)}, u32[]{:S(2)}, u32[]{:S(2)}) async-start(bf16[4,192,1600]{2,1,0:T(8,128)(2,1)} %bitcast.59), calls=%async_computation.11 | async-start | bytes 5111808 | tf_op jit(solution)/shard_map/all_to_all | solution.py:439
  621.2 213.0 %all-gather.16.cloned.1.call-start = ((), (), s32[]{:S(2)}) async-start(), calls=%async_computation.18 | async-start | bytes 3194880 | tf_op jit(solution)/shard_map/all_gather | solution.py:73
  771.9 111.3 %all-gather.20.cloned.1.call-start = ((), (), s32[]{:S(2)}) async-start(), calls=%async_computation.21 | async-start | bytes 10616832 | tf_op jit(solution)/shard_map/all_gather | solution.py:386
  842.6 39.1 %copy-start.92 = (f32[768,16]{0,1:T(8,128)}, f32[768,16]{0,1:T(8,128)S(1)}, u32[]{:S(2)}) copy-start(f32[768,16]{0,1:T(8,128)S(1)} %get-tuple-element.296) | copy-start | bytes 147460
  844.0 36.5 %copy-start.106 = (f32[768]{0:T(1024)}, f32[768]{0:T(1024)S(1)}, u32[]{:S(2)}) copy-start(f32[768]{0:T(1024)S(1)} %get-tuple-element.299) | copy-start | bytes 9220
  845.3 35.8 %copy-start.107 = (f32[768]{0:T(1024)}, f32[768]{0:T(1024)S(1)}, u32[]{:S(2)}) copy-start(f32[768]{0:T(1024)S(1)} %get-tuple-element.301) | copy-start | bytes 9220
  910.4 9.5 %copy-start.28 = (f32[2,768,512]{2,1,0:T(8,128)S(1)}, f32[2,768,512]{2,1,0:T(8,128)}, u32[]{:S(2)}) copy-start(f32[2,768,512]{2,1,0:T(8,128)} %get-tuple-element.302) | copy-start | bytes 9437188
  (114 other events, 324.8 us)
Sparse Core Ops, SparseCore 0:
  150.1 10.7 all-gather.9
  163.7 77.3 all-gather.7
  325.4 10.7 all-gather.11
  433.8 62.3 all-gather.17
  573.2 32.5 all-gather.13
  608.0 158.6 all-reduce.5
  772.0 25.4 all-gather.15
  823.3 17.9 all-gather.19

commit v2 on v1

v2 whole, which is shorter than its diff:
```python
import functools

import jax
import jax.numpy as jnp
from jax import lax
from jax.experimental import pallas as pl
from jax.experimental.pallas import tpu as pltpu
from jax.sharding import Mesh
from jax.sharding import PartitionSpec as P

D = 768
HEADS = 12
HEAD_DIM = 64
FF = 2048

highest = lax.Precision.HIGHEST
bf16 = jnp.bfloat16
f32 = jnp.float32
norm_eps = 1e-06
rope_base = 10000.0
masked_score = -1e30
ns_first = 3.4445
ns_second = -4.775
ns_third = 2.0315
decay_rate = 0.5
gain_rate = 0.05
router_rate = 0.02

DP = ("z", "y")
MP = ("x", "c")
SPARE = 64
SWAP = ((0, 1), (1, 0))
BLOCK = 256
VMEM_BYTES = 56 * 1024 * 1024


def rms_scale(values):
    return lax.rsqrt(jnp.mean(values * values, axis=-1, keepdims=True) + norm_eps)


def rotate(values, cosine, sine_part):
    half_dim = values.shape[-1] // 2
    first_half = values[..., :half_dim]
    second = values[..., half_dim:]
    return jnp.concatenate(
        [first_half * cosine - second * sine_part, second * cosine + first_half * sine_part],
        axis=-1,
    )


def swiglu_back(gate_values, up_values, grad_inner):
    sigmoid_gate = jax.nn.sigmoid(gate_values)
    grad_gate_part = (
        grad_inner * up_values * sigmoid_gate * (1.0 + gate_values * (1.0 - sigmoid_gate))
    )
    grad_up_part = grad_inner * gate_values * sigmoid_gate
    return grad_gate_part.astype(bf16), grad_up_part.astype(bf16)


def norm_back(grad_normed, inputs, row_scale, norm_gain):
    scaled = grad_normed * norm_gain
    return row_scale * scaled - inputs * row_scale**3 * jnp.mean(
        scaled * inputs, axis=-1, keepdims=True
    )


def mm(left, right):
    return jnp.dot(left, right, preferred_element_type=f32)


def mm_t(left, right):
    return lax.dot_general(left, right, (((1,), (1,)), ((), ())), preferred_element_type=f32)


def t_mm(left, right):
    return lax.dot_general(left, right, (((0,), (0,)), ((), ())), preferred_element_type=f32)


def two_parts(values):
    high = lax.reduce_precision(values, exponent_bits=8, mantissa_bits=7)
    return high.astype(bf16), (values - high).astype(bf16)


def swap_cores(values):
    return lax.ppermute(values, "c", SWAP)


def swap_chips(values):
    return lax.ppermute(values, "x", SWAP)


def swap_groups(values, distance):
    size = lax.axis_size(DP)
    return lax.ppermute(values, DP, [(place, place ^ distance) for place in range(size)])


def few_groups():
    return lax.axis_size(DP) <= 8


def local_order(values, row_count):
    place = lax.axis_index(MP)
    blocks = [
        lax.dynamic_slice_in_dim(values, (place ^ flip) * row_count, row_count, 0)
        for flip in (0, 2, 1, 3)
    ]
    return jnp.concatenate(blocks, axis=0)


def turn_pair(values):
    half = values.shape[0] // 2
    return jnp.concatenate([values[half:], values[:half]], axis=0)


def reduce_rows(partial):
    half = partial.shape[0] // 2
    got = swap_cores(partial[half:].astype(bf16))
    mine = (partial[:half] + got.astype(f32)).astype(bf16)
    return mine.astype(f32) + turn_pair(swap_chips(mine)).astype(f32)


def join_rows(rows):
    return jnp.concatenate([rows, swap_cores(rows)], axis=0)


def gather_shards(values):
    if not few_groups():
        return lax.all_gather(values, DP, axis=0, tiled=True)
    size = lax.axis_size(DP)
    place = lax.axis_index(DP)
    rows = values.shape[0]
    full = jnp.zeros((size * rows, values.shape[1]), values.dtype)
    full = lax.dynamic_update_slice_in_dim(full, values, place * rows, 0)
    for distance in range(1, size):
        got = swap_groups(values, distance)
        full = lax.dynamic_update_slice_in_dim(full, got, (place ^ distance) * rows, 0)
    return full


def scatter_shards(values):
    parts = lax.all_to_all(values.astype(bf16), DP, split_axis=0, concat_axis=0, tiled=True)
    return jnp.sum(parts.reshape(lax.axis_size(DP), -1, values.shape[1]).astype(f32), axis=0)


def exchange(values):
    return lax.all_to_all(values, DP, split_axis=0, concat_axis=0, tiled=True)


def paired_view(values):
    count, width, _, units = values.shape
    tiles = units // 128
    return (
        values.reshape(count, width, 2, tiles, 128)
        .transpose(0, 1, 3, 2, 4)
        .reshape(count, width * 2 * tiles, 128)
    )


def split_kernel(values_ref, out_ref, *, tiles, rows):
    for place in range(2 * tiles):
        column = (place % 2) * tiles * 128 + (place // 2) * 128
        out_ref[:, column : column + 128] = values_ref[
            pl.ds(place, rows, stride=2 * tiles), :
        ].astype(bf16)


def split_pairs(values):
    count, width, _, units = values.shape
    tiles = units // 128
    rows = BLOCK
    return pl.pallas_call(
        functools.partial(split_kernel, tiles=tiles, rows=rows),
        grid=(count, width // rows),
        in_specs=[pl.BlockSpec((None, rows * 2 * tiles, 128), lambda i, j: (i, j, 0))],
        out_specs=pl.BlockSpec((None, rows, 2 * units), lambda i, j: (i, j, 0)),
        out_shape=jax.ShapeDtypeStruct((count, width, 2 * units), bf16),
        name="split_pairs",
    )(paired_view(values))


def gram_term(matrix):
    width = matrix.shape[0]
    return jnp.concatenate(
        [
            mm_t(matrix[start : start + BLOCK], matrix[start:]).astype(bf16)
            for start in range(0, width, BLOCK)
        ],
        axis=1,
    )


def step_kernel(mine_ref, other_ref, step_ref, inverse_ref, gram):
    width = gram.shape[0]
    total = mine_ref[0].astype(f32) + other_ref[0].astype(f32)
    row = lax.broadcasted_iota(jnp.int32, (BLOCK, BLOCK), 0)
    column = lax.broadcasted_iota(jnp.int32, (BLOCK, BLOCK), 1)
    place = 0
    trace = jnp.zeros((1, 1), f32)
    for start in range(0, width, BLOCK):
        for across in range(start, width, BLOCK):
            block = total[:, place : place + BLOCK]
            place += BLOCK
            gram[start : start + BLOCK, across : across + BLOCK] = block
            if across > start:
                gram[across : across + BLOCK, start : start + BLOCK] = block.T
            else:
                diagonal = jnp.where(row == column, block, 0.0)
                trace += jnp.sum(jnp.sum(diagonal, axis=1, keepdims=True), axis=0, keepdims=True)
    inverse = 1.0 / (trace + 1e-12)
    first_gram = gram[...] * inverse
    first_low = first_gram.astype(bf16)
    first_poly = (ns_second * first_gram + ns_third * mm(first_low, first_low)).astype(bf16)
    mixed = mm(first_poly, first_low)
    second_gram = (
        ns_first * ns_first * first_gram
        + 2.0 * ns_first * mixed
        + mm(mixed.astype(bf16), first_poly)
    )
    second_low = second_gram.astype(bf16)
    second_poly = (ns_second * second_gram + ns_third * mm(second_low, second_low)).astype(bf16)
    combined = ns_first * (first_poly.astype(f32) + second_poly.astype(f32)) + mm(
        second_poly, first_poly
    )
    step_ref[0] = combined.astype(bf16)
    inverse_ref[0] = jnp.broadcast_to(inverse, (8, 128))


def step_matrices(mine, other):
    count, _, packed = mine.shape
    width = 768
    spec = pl.BlockSpec((1, BLOCK, packed), lambda i: (i, 0, 0))
    steps, inverse = pl.pallas_call(
        step_kernel,
        grid=(count,),
        in_specs=[spec, spec],
        out_specs=[
            pl.BlockSpec((1, width, width), lambda i: (i, 0, 0)),
            pl.BlockSpec((1, 8, 128), lambda i: (i, 0, 0)),
        ],
        out_shape=[
            jax.ShapeDtypeStruct((count, width, width), bf16),
            jax.ShapeDtypeStruct((count, 8, 128), f32),
        ],
        scratch_shapes=[pltpu.VMEM((width, width), f32)],
        compiler_params=pltpu.CompilerParams(vmem_limit_bytes=VMEM_BYTES),
        name="step_matrices",
    )(mine, other)
    return steps, inverse


def solve_steps(matrices):
    first_core = lax.axis_index("c") == 0
    half = len(matrices) // 2
    grams = [gram_term(matrix) for matrix in matrices]
    early, late = jnp.stack(grams[:half]), jnp.stack(grams[half:])
    got = swap_cores(jnp.where(first_core, late, early))
    mine = (jnp.where(first_core, early, late).astype(f32) + got.astype(f32)).astype(bf16)
    steps, inverse = step_matrices(mine, swap_chips(mine))
    other_steps, other_inverse = swap_cores(steps), swap_cores(inverse)
    early_steps = jnp.where(first_core, steps, other_steps)
    late_steps = jnp.where(first_core, other_steps, steps)
    early_inverse = jnp.where(first_core, inverse, other_inverse)
    late_inverse = jnp.where(first_core, other_inverse, inverse)
    return [
        (pair[0][index], pair[1][index, 0, 0])
        for pair in ((early_steps, early_inverse), (late_steps, late_inverse))
        for index in range(half)
    ]


def normed_delta(moment, step_rate):
    return -step_rate * moment * lax.rsqrt(jnp.mean(moment * moment) + 1e-12)


def local(
    tokens,
    teacher,
    segments,
    valid_mask,
    routes,
    first_gain,
    second_gain,
    router_weight,
    attention_in,
    attention_out,
    dense_in,
    dense_out,
    expert_in,
    expert_out,
    moment_first_gain,
    moment_second_gain,
    moment_router,
    moment_attention_in,
    moment_attention_out,
    moment_dense_in,
    moment_dense_out,
    moment_expert_in,
    moment_expert_out,
):
    row_count, width = tokens.shape
    mp_ways = lax.axis_size(MP)
    dp_ways = lax.axis_size(DP)
    dp_place = lax.axis_index(DP)
    chip_place = lax.axis_index("x")
    core_place = lax.axis_index("c")
    first_core = core_place == 0
    seq_len = row_count * mp_ways
    expert_total = router_weight.shape[1]
    capacity = 4 * seq_len // expert_total
    half_cap = capacity // 2
    shard_rows = attention_in.shape[0]
    slabs = expert_in.shape[0]
    units = expert_in.shape[3]
    dense_units = dense_in.shape[2]
    sharing = FF // (units * mp_ways)
    heads_here = attention_in.shape[2] // HEAD_DIM
    head_cols = attention_in.shape[2]
    project_cols = 3 * head_cols
    project_scale = (3 * HEADS * HEAD_DIM / D) ** 0.5
    mix_scale = (HEADS * HEAD_DIM / D) ** 0.5
    pair_scale = (2 * FF / D) ** 0.5
    single_scale = (FF / D) ** 0.5
    slab_pair_scale = (2 * FF / (sharing * D)) ** 0.5
    slab_single_scale = (FF / (sharing * D)) ** 0.5
    by_slab = few_groups() and slabs % 2 == 0 and sharing == 1
    group = slabs // 2 if by_slab else slabs

    mask_float = valid_mask.astype(f32)
    own_count = jnp.sum(mask_float)
    high_count = jnp.floor(own_count / 256.0)
    count_cells = jnp.zeros((shard_rows, SPARE), f32)
    count_cells = count_cells.at[0, 0].set(high_count)
    count_cells = count_cells.at[1, 0].set(own_count - 256.0 * high_count)
    first_pack = jnp.concatenate(
        [attention_in.reshape(shard_rows, project_cols), count_cells, attention_out], axis=1
    ).astype(bf16)
    first_full = gather_shards(first_pack)
    weight_project = first_full[:, :project_cols]
    weight_mix = first_full[:, project_cols + SPARE :]
    counts = first_full[:, project_cols].astype(f32).reshape(dp_ways, shard_rows)
    valid_count = jnp.sum(256.0 * counts[:, 0] + counts[:, 1])
    tokens_pair = jnp.concatenate([tokens, swap_chips(tokens)], axis=0)
    teacher_pair = jnp.concatenate([teacher, swap_chips(teacher)], axis=0)
    second_pack = jnp.concatenate(
        [dense_in[:, 0, :], dense_in[:, 1, :], dense_out], axis=1
    ).astype(bf16)
    second_full = gather_shards(second_pack)
    weight_pair = second_full[:, : 2 * dense_units]
    weight_down = second_full[:, 2 * dense_units :]
    router_low = router_weight.astype(bf16)
    expert_pair = split_pairs(expert_in)
    expert_down = expert_out.astype(bf16)
    if by_slab:
        kept = lax.dynamic_slice_in_dim(expert_pair, core_place * group, group, 0)
        sent = lax.dynamic_slice_in_dim(expert_pair, (1 - core_place) * group, group, 0)
        got = swap_cores(sent)
        expert_gate = jnp.concatenate([kept[:, :, :units], got[:, :, :units]], axis=2)
        expert_up = jnp.concatenate([kept[:, :, units:], got[:, :, units:]], axis=2)
        kept = lax.dynamic_slice_in_dim(expert_down, core_place * group, group, 0)
        sent = lax.dynamic_slice_in_dim(expert_down, (1 - core_place) * group, group, 0)
        expert_down = jnp.concatenate([kept, swap_cores(sent)], axis=2)
    else:
        expert_gate = expert_pair[:, :, :units]
        expert_up = expert_pair[:, :, units:]

    order = local_order(jnp.arange(seq_len, dtype=jnp.int32), row_count)
    names = local_order(routes, row_count)
    documents = local_order(segments, row_count)
    onehot = (
        names[:, :, None] == jnp.arange(expert_total, dtype=jnp.int32)[None, None, :]
    ).astype(f32)
    earlier = mm(
        (order[:, None] > order[None, :]).astype(bf16), jnp.sum(onehot, axis=1).astype(bf16)
    )
    ranks = jnp.sum(onehot * earlier[:, None, :], axis=-1).astype(jnp.int32)
    if by_slab:
        half_ranks = ranks - chip_place * half_cap
        lanes = names % slabs
        here = lanes // group == core_place
        slot_rows = ((names // slabs) ^ dp_place) * group + lanes % group
        slot_total = dp_ways * group * half_cap
    else:
        half_ranks = ranks - core_place * half_cap
        here = True
        slot_rows = names
        slot_total = expert_total * half_cap
    here = here & (half_ranks >= 0) & (half_ranks < half_cap)
    slot_ids = jnp.where(here, slot_rows * half_cap + half_ranks, -1)
    slot_order = jnp.arange(slot_total, dtype=jnp.int32)
    picks = [(slot_ids[:, k][:, None] == slot_order[None, :]) for k in range(2)]
    select = (picks[0] | picks[1]).astype(bf16)

    def to_owners(rows):
        if by_slab:
            chunks = rows.reshape(dp_ways, group * half_cap, width)
            mine, other = [chunks[0]], []
            for distance in range(1, dp_ways):
                mine.append(swap_groups(chunks[distance], distance))
            for chunk in mine:
                other.append(swap_chips(chunk))
            whole = jnp.stack(mine + other).reshape(2 * dp_ways, group, half_cap, width)
            return [whole[:, slab].reshape(-1, width) for slab in range(group)]
        spread = jnp.broadcast_to(
            rows.reshape(expert_total, 1, half_cap, width),
            (expert_total, sharing, half_cap, width),
        ).reshape(expert_total * sharing, half_cap, width)
        moved = exchange(spread).reshape(dp_ways, slabs, half_cap, width)
        both = lax.all_gather(moved, "c", axis=0)
        return [both[:, :, slab].reshape(-1, width) for slab in range(slabs)]

    def to_sources(parts):
        if by_slab:
            whole = jnp.stack(
                [part.reshape(2, dp_ways, half_cap, width) for part in parts], axis=2
            )
            step = 2 if dp_ways > 2 else 1
            back = []
            for start in range(0, dp_ways, step):
                got = swap_chips(whole[1, start : start + step].astype(bf16))
                total = (whole[0, start : start + step].astype(f32) + got.astype(f32)).astype(bf16)
                for distance in range(start, start + step):
                    chunk = total[distance - start]
                    back.append(swap_groups(chunk, distance) if distance else chunk)
            return jnp.stack(back).reshape(slot_total, width)
        stacked = jnp.stack(
            [part.reshape(2, dp_ways, half_cap, width) for part in parts], axis=2
        ).astype(bf16)
        swapped = lax.all_to_all(stacked, "c", split_axis=0, concat_axis=0, tiled=True)
        halves = (swapped[0].astype(f32) + swapped[1].astype(f32)).astype(bf16)
        moved = exchange(halves.reshape(dp_ways * slabs, half_cap, width))
        moved = moved.reshape(expert_total, sharing, half_cap, width)
        if sharing > 1:
            moved = jnp.sum(moved.astype(f32), axis=1).astype(bf16)
        return moved.reshape(slot_total, width)

    token_float = tokens_pair.astype(f32)
    scale_one = rms_scale(token_float)
    full_one = join_rows((token_float * scale_one * first_gain).astype(bf16))
    projected = mm(full_one, weight_project).reshape(seq_len, 3, heads_here, HEAD_DIM)
    frequency = rope_base ** (-jnp.arange(HEAD_DIM // 2, dtype=f32) * 2.0 / HEAD_DIM)
    angles = order.astype(f32)[:, None] * frequency[None, :]
    cosine = jnp.cos(angles)[:, None, :]
    sine = jnp.sin(angles)[:, None, :]
    query_scale = HEAD_DIM ** (-0.5)
    queries = (rotate(projected[:, 0], cosine, sine) * query_scale).astype(bf16)
    key_rows = rotate(projected[:, 1], cosine, sine).astype(bf16)
    value_rows = projected[:, 2].astype(bf16)
    allowed = (documents[:, None] == documents[None, :]) & (order[:, None] >= order[None, :])

    def head_scores():
        scores = jnp.einsum("qhd,khd->hqk", queries, key_rows, preferred_element_type=f32)
        return jnp.where(allowed[None], scores, masked_score)

    scores = head_scores()
    row_peak = jnp.max(scores, axis=-1, keepdims=True)
    exponent = jnp.exp(scores - row_peak)
    row_total = jnp.sum(exponent, axis=-1, keepdims=True)
    probs = exponent / row_total
    probs_low = probs.astype(bf16)
    mixed_low = (
        jnp.einsum("hqk,khd->qhd", probs_low, value_rows, preferred_element_type=f32)
        .astype(bf16)
        .reshape(seq_len, head_cols)
    )
    log_totals = row_peak + jnp.log(row_total)
    hidden = token_float + reduce_rows(mm_t(mixed_low, weight_mix))
    scale_two = rms_scale(hidden)
    full_two = join_rows((hidden * scale_two * second_gain).astype(bf16))

    received = to_owners(t_mm(select, full_two).astype(bf16))

    gate_up = mm(full_two, weight_pair)
    gate_part = gate_up[:, :dense_units]
    up_part = gate_up[:, dense_units:]
    dense_inner = (jax.nn.silu(gate_part) * up_part).astype(bf16)
    dense_part = mm_t(dense_inner, weight_down)
    logits = mm(full_two, router_low)
    chosen = jnp.sum(onehot * logits[:, None, :], axis=-1)
    gate_probs = jax.nn.softmax(chosen, axis=-1)
    weighted = (
        jnp.where(picks[0], gate_probs[:, 0:1], 0.0) + jnp.where(picks[1], gate_probs[:, 1:2], 0.0)
    ).astype(bf16)

    slab_gate, slab_up, slab_inner, slab_parts = [], [], [], []
    for slab in range(group):
        gate_values = mm(received[slab], expert_gate[slab])
        up_values = mm(received[slab], expert_up[slab])
        inner = (jax.nn.silu(gate_values) * up_values).astype(bf16)
        slab_gate.append(gate_values)
        slab_up.append(up_values)
        slab_inner.append(inner)
        slab_parts.append(mm_t(inner, expert_down[slab]).astype(bf16))
    expert_rows = to_sources(slab_parts)
    output = hidden + reduce_rows(dense_part + mm(weighted, expert_rows))
    errors = output - teacher_pair.astype(f32)
    pair_mask = local_order(mask_float, row_count)[: 2 * row_count]
    loss_local = jnp.sum(jnp.sum(errors * errors, axis=-1)[:row_count] * pair_mask[:row_count])
    factor = seq_len * dp_ways / valid_count
    grad_output = errors * (pair_mask * factor)[:, None]
    grad_branch = join_rows(grad_output.astype(bf16))

    raw_slots = t_mm(select, grad_branch)
    slot_gates = jnp.sum(
        jnp.where(picks[0], gate_probs[:, 0:1], 0.0) + jnp.where(picks[1], gate_probs[:, 1:2], 0.0),
        axis=0,
    )
    grad_received = to_owners((raw_slots * slot_gates[:, None]).astype(bf16))
    slot_dots = jnp.sum(raw_slots * expert_rows.astype(f32), axis=-1)
    grad_chosen_raw = jnp.stack(
        [jnp.sum(jnp.where(pick, slot_dots[None, :], 0.0), axis=-1) for pick in picks], axis=-1
    )
    grad_chosen = gate_probs * (
        grad_chosen_raw - jnp.sum(gate_probs * grad_chosen_raw, axis=-1, keepdims=True)
    )
    grad_logits = jnp.sum(onehot * grad_chosen[:, :, None], axis=1)
    logits_high, logits_rest = two_parts(grad_logits)
    grad_router = t_mm(full_two, logits_high) + t_mm(full_two, logits_rest)

    grad_dense_inner = mm(grad_branch, weight_down)
    grad_gate, grad_up = swiglu_back(gate_part, up_part, grad_dense_inner)
    grad_pair = jnp.concatenate([grad_gate, grad_up], axis=1)
    grad_down = t_mm(grad_branch, dense_inner)
    grad_dense_in = t_mm(full_two, grad_pair)
    grad_full_two = (
        mm_t(grad_pair, weight_pair) + mm_t(logits_high, router_low) + mm_t(logits_rest, router_low)
    )

    slab_dispatch, grad_in_slabs, grad_out_slabs = [], [], []
    for slab in range(group):
        grad_inner = mm(grad_received[slab], expert_down[slab])
        grad_g, grad_u = swiglu_back(slab_gate[slab], slab_up[slab], grad_inner)
        slab_dispatch.append(
            (mm_t(grad_g, expert_gate[slab]) + mm_t(grad_u, expert_up[slab])).astype(bf16)
        )
        grad_in_slabs.append((t_mm(received[slab], grad_g), t_mm(received[slab], grad_u)))
        grad_out_slabs.append(t_mm(grad_received[slab], slab_inner[slab]))
    grad_slot_rows = to_sources(slab_dispatch)
    grad_normed_two = reduce_rows(grad_full_two + mm(select, grad_slot_rows))
    dense_shard = scatter_shards(jnp.concatenate([grad_dense_in, grad_down], axis=1))

    if by_slab:
        stacked = jnp.stack(
            [
                jnp.concatenate([gate_grad, up_grad, down_grad], axis=1)
                for (gate_grad, up_grad), down_grad in zip(grad_in_slabs, grad_out_slabs)
            ]
        ).reshape(group, width, 3, 2, units)
        kept = stacked[:, :, :, 0]
        got = swap_cores(stacked[:, :, :, 1].astype(bf16)).astype(f32)
        both = jnp.concatenate(
            [jnp.where(first_core, kept, got), jnp.where(first_core, got, kept)], axis=0
        )
        grad_expert_in = both[:, :, :2]
        grad_expert_out = both[:, :, 2]
    else:
        grad_expert_in = jnp.stack([jnp.stack(pair, axis=1) for pair in grad_in_slabs])
        grad_expert_out = jnp.stack(grad_out_slabs)
    new_moment_expert_in = decay_rate * moment_expert_in + grad_expert_in
    new_moment_expert_out = decay_rate * moment_expert_out + grad_expert_out
    expert_matrices = []
    for slab in range(slabs):
        expert_matrices.append(
            jnp.concatenate(
                [new_moment_expert_in[slab, :, 0, :], new_moment_expert_in[slab, :, 1, :]], axis=1
            ).astype(bf16)
        )
        expert_matrices.append(new_moment_expert_out[slab].astype(bf16))
    expert_steps = solve_steps(expert_matrices)
    shard_pair = dense_shard[:, : 2 * dense_units].reshape(shard_rows, 2, dense_units)
    shard_down = dense_shard[:, 2 * dense_units :]
    new_moment_pair = decay_rate * moment_dense_in + shard_pair
    new_moment_down = decay_rate * moment_dense_out + shard_down
    dense_moments = lax.all_gather(
        jnp.concatenate(
            [new_moment_pair[:, 0, :], new_moment_pair[:, 1, :], new_moment_down], axis=1
        ).astype(bf16),
        DP,
        axis=0,
        tiled=True,
    )
    full_pair = dense_moments[:, : 2 * dense_units]
    full_down = dense_moments[:, 2 * dense_units :]
    dense_steps = solve_steps([full_pair, full_down])

    grad_hidden = norm_back(grad_normed_two, hidden, scale_two, second_gain) + grad_output
    grad_second_part = jnp.sum((grad_normed_two * hidden * scale_two)[:row_count], axis=0)
    grad_attended = join_rows(grad_hidden.astype(bf16))
    grad_mix = t_mm(grad_attended, mixed_low)
    grad_mixed = (
        mm(grad_attended, weight_mix).astype(bf16).reshape(seq_len, heads_here, HEAD_DIM)
    )
    score_weights = jnp.exp(head_scores() - log_totals)
    grad_weights = jnp.einsum("qhd,khd->hqk", grad_mixed, value_rows, preferred_element_type=f32)
    row_dots = jnp.sum(grad_weights * score_weights, axis=-1, keepdims=True)
    grad_scores = (score_weights * (grad_weights - row_dots)).astype(bf16)
    grad_queries = jnp.einsum("hqk,khd->qhd", grad_scores, key_rows, preferred_element_type=f32)
    grad_keys = jnp.einsum("hqk,qhd->khd", grad_scores, queries, preferred_element_type=f32)
    grad_values = jnp.einsum(
        "hqk,qhd->khd", score_weights.astype(bf16), grad_mixed, preferred_element_type=f32
    )
    grad_projected = jnp.concatenate(
        [
            rotate(grad_queries * query_scale, cosine, -sine).reshape(seq_len, head_cols),
            rotate(grad_keys, cosine, -sine).reshape(seq_len, head_cols),
            grad_values.reshape(seq_len, head_cols),
        ],
        axis=1,
    ).astype(bf16)
    grad_project = t_mm(full_one, grad_projected)
    grad_full_one = mm_t(grad_projected, weight_project)
    grad_first_part = jnp.sum(grad_full_one * full_one.astype(f32), axis=0) / first_gain

    loss_cells = jnp.zeros((width, 1), f32).at[0, 0].set(loss_local)
    small = jnp.concatenate(
        [grad_first_part[:, None], grad_second_part[:, None], grad_router, loss_cells], axis=1
    )
    small = jnp.pad(small, ((0, 0), (0, SPARE // 2 - small.shape[1])))
    small = jnp.concatenate(two_parts(small), axis=1)
    last_shard = scatter_shards(jnp.concatenate([grad_project.astype(bf16), small, grad_mix.astype(bf16)], axis=1))
    shard_project = last_shard[:, :project_cols].reshape(shard_rows, 3, head_cols)
    shard_mix = last_shard[:, project_cols + SPARE :]
    new_moment_project = decay_rate * moment_attention_in + shard_project
    new_moment_mix = decay_rate * moment_attention_out + shard_mix
    small = last_shard[:, project_cols : project_cols + SPARE // 2]
    small = small + last_shard[:, project_cols + SPARE // 2 : project_cols + SPARE]
    last_moments = gather_shards(
        jnp.concatenate(
            [
                new_moment_project.reshape(shard_rows, project_cols).astype(bf16),
                *two_parts(small),
                new_moment_mix.astype(bf16),
            ],
            axis=1,
        )
    )
    full_project = last_moments[:, :project_cols]
    full_mix = last_moments[:, project_cols + SPARE :]
    last_steps = solve_steps([full_project, full_mix])
    small_pair = last_moments[:, project_cols : project_cols + SPARE].astype(f32)
    small_part = small_pair[:, : SPARE // 2] + small_pair[:, SPARE // 2 :]
    small_part = small_part + swap_cores(small_part)
    small_total = small_part + swap_chips(small_part)
    grad_normed_one = reduce_rows(grad_full_one)
    grad_tokens = norm_back(grad_normed_one, token_float, scale_one, first_gain) + grad_hidden

    first_total = small_total[:, 0]
    second_total = small_total[:, 1]
    router_total = small_total[:, 2 : 2 + expert_total]
    loss_total = small_total[0, 2 + expert_total]
    loss_value = loss_total / (valid_count * width)
    new_moment_first = decay_rate * moment_first_gain + first_total
    new_moment_second = decay_rate * moment_second_gain + second_total
    new_moment_router = decay_rate * moment_router + router_total

    def update(solved, matrix, step_scale):
        step, inverse = solved
        full = ns_first * ns_first * matrix.astype(f32) + mm(step, matrix)
        return (-step_scale * jnp.sqrt(inverse)) * full

    def update_rows(solved, matrix, step_scale):
        step, inverse = solved
        step_rows = lax.dynamic_slice_in_dim(step, dp_place * shard_rows, shard_rows, 0)
        own_rows = lax.dynamic_slice_in_dim(matrix, dp_place * shard_rows, shard_rows, 0)
        full = ns_first * ns_first * own_rows.astype(f32) + mm(step_rows, matrix)
        return (-step_scale * jnp.sqrt(inverse)) * full

    step_first = normed_delta(new_moment_first, gain_rate)
    step_second = normed_delta(new_moment_second, gain_rate)
    new_router = router_weight + normed_delta(new_moment_router, router_rate)
    new_attention_in = attention_in + update_rows(
        last_steps[0], full_project, project_scale
    ).reshape(attention_in.shape)
    step_mix = update_rows(last_steps[1], full_mix, mix_scale)
    new_dense_in = dense_in + update_rows(dense_steps[0], full_pair, pair_scale).reshape(
        dense_in.shape
    )
    new_dense_out = dense_out + update_rows(dense_steps[1], full_down, single_scale)
    pair_steps, single_steps = [], []
    for slab in range(slabs):
        pair_steps.append(
            update(expert_steps[2 * slab], expert_matrices[2 * slab], slab_pair_scale).reshape(
                width, 2, units
            )
        )
        single_steps.append(
            update(expert_steps[2 * slab + 1], expert_matrices[2 * slab + 1], slab_single_scale)
        )
    new_expert_in = expert_in + jnp.stack(pair_steps)
    new_expert_out = expert_out + jnp.stack(single_steps)
    return (
        output[:row_count].astype(bf16),
        loss_value,
        grad_tokens[:row_count],
        first_total,
        second_total,
        router_total,
        shard_project,
        shard_mix,
        shard_pair,
        shard_down,
        grad_expert_in,
        grad_expert_out,
        new_moment_first,
        new_moment_second,
        new_moment_router,
        new_moment_project,
        new_moment_mix,
        new_moment_pair,
        new_moment_down,
        new_moment_expert_in,
        new_moment_expert_out,
        step_first,
        step_second,
        new_router,
        new_attention_in,
        step_mix,
        new_dense_in,
        new_dense_out,
        new_expert_in,
        new_expert_out,
    )


def solution(mesh):
    dp_ways, mp_ways = mesh.devices.shape
    fine_mesh = Mesh(
        mesh.devices.reshape(dp_ways // 2, 2, mp_ways // 2, 2), ("z", "y", "x", "c")
    )
    rows = P(("z", "y", "x", "c"), None)
    project = P(DP, None, MP)
    plain = P(DP, MP)
    slab_pair = P(DP, None, None, MP)
    slab_single = P(DP, None, MP)
    weights = (P(), P(), P(), project, plain, project, plain, slab_pair, slab_single)
    return jax.shard_map(
        local,
        mesh=fine_mesh,
        in_specs=(rows, rows, P(DP), P(DP), P(DP, None)) + weights + weights,
        out_specs=(rows, P(), rows) + weights + weights + weights,
        check_vma=False,
    )
```

time: 947 us -> 756 us (0.80)
  blocking collectives: 188 us -> 0 us
  waiting for transfers between devices: 267 us -> 155 us
  matrix products: 197 us -> 98.6 us
  starting transfers between devices: 43.9 us -> 136 us
  local copies, waits for them, and re-layouts: 114 us -> 185 us
  Pallas kernels: 0 us -> 34.8 us
    ppermute x0 -> x104, waiting for transfers between devices: none -> 151 us  [the longest x34 99.3 us: swap_chips(): return lax.ppermute(values, 'x', SWAP)]
    ppermute x0 -> x104, starting transfers between devices: none -> 126 us  [the longest x49 89.2 us: swap_groups(): lax.ppermute(values, DP, [(place, place ^ distance) for place in range(si...]
    psum x1 -> x0, waiting for transfers between devices: 114 us -> none  [local(): lax.psum(jnp.stack([gram_term(matrix) for matrix in early]), MP)]
    all_to_all x4 -> x0, blocking collectives: 96.8 us -> none  [the longest x2 83.3 us: exchange(): return lax.all_to_all(values, DP, split_axis=0, concat_axis=0, tiled=True)]
    all_gather x9 -> x0, blocking collectives: 88.9 us -> none  [the longest x2 37 us: gather_shards(): return lax.all_gather(paired, 'z', axis=0, tiled=True)]
    dot_general x10 -> x0, matrix products: 77.3 us -> none  [bmm(): return jnp.einsum('nij,njk->nik', left, right, preferred_element_type=f32)]
    all_gather x6 -> x0, waiting for transfers between devices: 66.7 us -> none  [the longest x1 50.9 us: local(): second_full = lax.all_gather(second_pack, DP, axis=0, tiled=True)]
    dynamic_update_slice x0 -> x23, local copies, waits for them, and re-layouts: none -> 63.4 us  [the longest x21 57.6 us: gather_shards(): lax.dynamic_update_slice_in_dim(full, got, (place ^ distance) * rows, 0)]
  transfers between devices with their start and end apart: 18 -> 107, of which waited for: 11 -> 41; matrix products, arithmetic and copies ran while one was open for 32% -> 44% of each run, Pallas kernels for 0% -> 4%
where the time goes in v2:
time: 756 us; the launch traced here: 744 us
  local copies, waits for them, and re-layouts  185 us (24%)
  waiting for transfers between devices  155 us (21%)
  starting transfers between devices  136 us (18%)
  other arithmetic  106 us (14%)
  matrix products  98.6 us (13%)
  Pallas kernels  34.8 us (5%)
  between operations  29.6 us (4%)
    ppermute x34, waiting for transfers between devices, swap_chips(): return lax.ppermute(values, 'x', SWAP)  99.3 us
    ppermute x49, starting transfers between devices, swap_groups(): lax.ppermute(values, DP, [(place, place ^ distance) for place in range(si...  89.2 us
    dynamic_update_slice x21, local copies, waits for them, and re-layouts, gather_shards(): lax.dynamic_update_slice_in_dim(full, got, (place ^ distance) * rows, 0)  57.6 us
    unnamed x445, local copies, waits for them, and re-layouts  54.3 us
    ppermute x49, waiting for transfers between devices, swap_groups(): lax.ppermute(values, DP, [(place, place ^ distance) for place in range(si...  49.7 us
    dot_general x33, matrix products, mm_t(): lax.dot_general(left, right, (((1,), (1,)), ((), ())), preferred_element_...  38.3 us
    dot_general x19, matrix products, mm(): return jnp.dot(left, right, preferred_element_type=f32)  35.3 us
    ppermute x34, starting transfers between devices, swap_chips(): return lax.ppermute(values, 'x', SWAP)  33.6 us
  transfers between devices with their start and end apart: 107, of which 41 were waited for; matrix products, arithmetic and copies ran while one was open for 44% of the time, Pallas kernels for 4%

profile of v2, /device:TPU:0, one launch (start us, length us, event | category | flops | bytes accessed | tf_op | source)
XLA Modules:
  0.0 744.4 jit_solution(17294864301086888926)
XLA Ops:
  22.9 6.5 split_pairs.1
  38.7 3.6 collective-permute-start.7
  53.4 3.7 dynamic_update_slice.73
  57.1 3.7 dynamic_update_slice.74
  60.8 3.7 dynamic_update_slice.75
  69.5 3.7 dynamic_update_slice.77
  75.6 3.7 dynamic_update_slice.78
  81.1 3.8 dynamic_update_slice.79
  89.7 3.6 collective-permute-start.17
  103.2 10.9 %collective-permute-done.15 = bf16[96,1536]{1,0:T(8,128)(2,1)} collective-permute-done((bf16[96,1536]{1,0:T(8,128)(2,1)}, bf16[96,1536]{1,0:T(8,128)(2,1)}, u32[]{:S(2)}, u32[]{:S(2)}) %collective-permute-start.15) | collective-permute-done | bytes 294944 | tf_op jit(solution)/shard_map/ppermute | solution.py:94
  116.4 3.8 collective-permute-done.16
  122.2 5.8 collective-permute-done.10
  178.1 4.0 multiply_convert_fusion.2
  190.0 3.7 collective-permute-done.41
  198.6 4.3 collective-permute-start.37
  233.9 4.9 collective-permute-done.48
  309.7 4.2 multiply_convert_fusion.1
  321.9 3.7 collective-permute-done.71
  325.6 4.2 collective-permute-done.68
  344.8 4.5 collective-permute-done.72
  360.1 6.6 collective-permute-done.78
  369.9 8.5 %pad_maximum_fusion = f32[768,3072]{1,0:T(8,128)} fusion(f32[768,1024]{1,0:T(8,128)} %fusion.245, f32[768,1024]{1,0:T(8,128)} %fusion.244, f32[768,1024]{1,0:T(8,128)} %fusion.243), kind=kLoop, calls=%fused_computation | loop fusion | flops 4718592 | bytes 18874368 | tf_op jit(solution)/shard_map/concatenate | solution.py:544
  378.4 13.1 %reshape_stack.3 = f32[1,768,3,2,512]{4,3,2,1,0:T(2,128)} reshape(f32[768,3072]{1,0:T(8,128)} %pad_maximum_fusion) | data formatting | bytes 18874368 | tf_op jit(solution)/shard_map/reshape;stack | solution.py:547
  391.5 6.7 slice.944
  412.0 4.3 slice.943
  422.5 5.0 all-to-all-start
  433.4 4.7 convert_select_fusion.1
  438.1 6.1 fusion.220
  456.5 3.8 all-to-all-done
  461.3 4.4 all-to-all-start.1
  468.4 10.5 %copy.330 = f32[2,768,2,512]{3,2,1,0:T(2,128)} copy(f32[2,768,2,512]{3,1,2,0:T(8,128)} %get-tuple-element.237) | data formatting | bytes 12582912
  478.9 7.6 %copy.334 = f32[2,768,2,512]{3,2,1,0:T(2,128)} copy(f32[2,768,2,512]{3,1,2,0:T(8,128)S(1)} %bitcast.432) | data formatting | bytes 12582912
  510.3 4.0 collective-permute-start.86
  520.6 3.7 dynamic_update_slice.89
  524.3 3.7 dynamic_update_slice.90
  528.1 3.7 dynamic_update_slice.91
  531.8 12.1 %collective-permute-done.83 = bf16[96,832]{0,1:T(8,128)(2,1)} collective-permute-done((bf16[96,832]{0,1:T(8,128)(2,1)S(1)}, bf16[96,832]{0,1:T(8,128)(2,1)}, u32[]{:S(2)}, u32[]{:S(2)}) %collective-permute-start.83) | collective-permute-done | bytes 159776 | tf_op jit(solution)/shard_map/ppermute | solution.py:94
  549.2 3.7 dynamic_update_slice.93
  552.9 3.7 dynamic_update_slice.94
  556.6 3.6 dynamic_update_slice.95
  594.3 40.2 %collective-permute-done.93.other_ref = bf16[1,256,1536]{2,1,0:T(8,128)(2,1)S(1)} collective-permute-done((bf16[1,256,1536]{2,1,0:T(8,128)(2,1)S(1)}, bf16[1,256,1536]{2,1,0:T(8,128)(2,1)S(1)}, u32[]{:S(2)}, u32[]{:S(2)}) %collective-permute-start.93) | collective-permute-done | bytes 786464 | tf_op jit(solution)/shard_map/ppermute | solution.py:89
  635.4 7.6 %step_matrices.3 = (bf16[1,768,768]{2,1,0:T(8,128)(2,1)}, f32[1,8,128]{2,1,0:T(8,128)}) custom-call(bf16[1,256,1536]{2,1,0:T(8,128)(2,1)} %copy-done.30, bf16[1,256,1536]{2,1,0:T(8,128)(2,1)} %copy-done.74), custom_call_target="tpu_custom_call" | custom-call | tf_op jit(solution)/shard_map/step_matrices/pallas_call | solution.py:232
  645.3 13.1 %step_matrices.5 = (bf16[2,768,768]{2,1,0:T(8,128)(2,1)}, f32[2,8,128]{2,1,0:T(8,128)}) custom-call(bf16[2,256,1536]{2,1,0:T(8,128)(2,1)} %add_convert_fusion.mine_ref, bf16[2,256,1536]{2,1,0:T(8,128)(2,1)} %collective-permute-done.101.other_ref), custom_call_target="tpu_custom_call" | custom-call | tf_op jit(solution)/shard_map/step_matrices/pallas_call | solution.py:232
  688.6 4.2 stack_reshape.15
  692.9 5.3 add_multiply_fusion.1
  698.2 5.7 stack_reshape.14
  704.7 7.6 %step_matrices.4 = (bf16[1,768,768]{2,1,0:T(8,128)(2,1)}, f32[1,8,128]{2,1,0:T(8,128)}) custom-call(bf16[1,256,1536]{2,1,0:T(8,128)(2,1)} %add_convert_fusion.2.mine_ref, bf16[1,256,1536]{2,1,0:T(8,128)(2,1)} %collective-permute-done.97.other_ref), custom_call_target="tpu_custom_call" | custom-call | tf_op jit(solution)/shard_map/step_matrices/pallas_call | solution.py:232
  712.3 9.5 %maximum_add_fusion = f32[2,768,2,512]{3,2,1,0:T(2,128)} fusion(f32[2,768,2,512]{3,2,1,0:T(2,128)} %param.41, f32[1,768,2,512]{3,2,1,0:T(2,128)S(1)} %stack_reshape.15, f32[1,768,2,512]{3,2,1,0:T(2,128)} %stack_reshape.14), kind=kLoop, calls=%fused_computation.4 | loop fusion | flops 3145728 | bytes 18874368 | tf_op jit(solution)/shard_map/add | solution.py:688
  (904 shorter events, 412.2 us)
Async XLA Ops:
  12.8 25.9 %collective-permute-start.2 = (bf16[96,832]{0,1:T(8,128)(2,1)}, bf16[96,832]{0,1:T(8,128)(2,1)}, u32[]{:S(2)}, u32[]{:S(2)}) collective-permute-start(bf16[96,832]{0,1:T(8,128)(2,1)} %pad_maximum_fusion.36), channel_id=1, source_target_pairs={{0,4},{4,0},{8,12},{12,8},{16,20},{20,16},{24,28},{28,24},{1,5},{5... | collective-permute-start | bytes 479240 | tf_op jit(solution)/shard_map/ppermute | solution.py:94
  15.8 26.6 %collective-permute-start.3 = (bf16[96,832]{0,1:T(8,128)(2,1)}, bf16[96,832]{0,1:T(8,128)(2,1)}, u32[]{:S(2)}, u32[]{:S(2)}) collective-permute-start(bf16[96,832]{0,1:T(8,128)(2,1)} %pad_maximum_fusion.36), channel_id=1, source_target_pairs={{0,8},{4,12},{8,0},{12,4},{16,24},{20,28},{24,16},{28,20},{1,9},{5... | collective-permute-start | bytes 479240 | tf_op jit(solution)/shard_map/ppermute | solution.py:94
  17.4 25.0 %collective-permute-start.4 = (bf16[96,832]{0,1:T(8,128)(2,1)}, bf16[96,832]{0,1:T(8,128)(2,1)}, u32[]{:S(2)}, u32[]{:S(2)}) collective-permute-start(bf16[96,832]{0,1:T(8,128)(2,1)} %pad_maximum_fusion.36), channel_id=1, source_target_pairs={{0,12},{4,8},{8,4},{12,0},{16,28},{20,24},{24,20},{28,16},{1,13},{... | collective-permute-start | bytes 479240 | tf_op jit(solution)/shard_map/ppermute | solution.py:94
  17.4 47.2 %collective-permute-start.5 = (bf16[96,832]{0,1:T(8,128)(2,1)}, bf16[96,832]{0,1:T(8,128)(2,1)}, u32[]{:S(2)}, u32[]{:S(2)}) collective-permute-start(bf16[96,832]{0,1:T(8,128)(2,1)} %pad_maximum_fusion.36), channel_id=1, source_target_pairs={{0,16},{4,20},{8,24},{12,28},{16,0},{20,4},{24,8},{28,12},{1,17},{... | collective-permute-start | bytes 479240 | tf_op jit(solution)/shard_map/ppermute | solution.py:94
  20.3 48.7 %collective-permute-start.6 = (bf16[96,832]{0,1:T(8,128)(2,1)}, bf16[96,832]{0,1:T(8,128)(2,1)}, u32[]{:S(2)}, u32[]{:S(2)}) collective-permute-start(bf16[96,832]{0,1:T(8,128)(2,1)} %pad_maximum_fusion.36), channel_id=1, source_target_pairs={{0,20},{4,16},{8,28},{12,24},{16,4},{20,0},{24,12},{28,8},{1,21},{... | collective-permute-start | bytes 479240 | tf_op jit(solution)/shard_map/ppermute | solution.py:94
  38.7 34.4 %collective-permute-start.7 = (bf16[96,832]{0,1:T(8,128)(2,1)}, bf16[96,832]{0,1:T(8,128)(2,1)}, u32[]{:S(2)}, u32[]{:S(2)}) collective-permute-start(bf16[96,832]{0,1:T(8,128)(2,1)} %pad_maximum_fusion.36), channel_id=1, source_target_pairs={{0,24},{4,28},{8,16},{12,20},{16,8},{20,12},{24,0},{28,4},{1,25},{... | collective-permute-start | bytes 479240 | tf_op jit(solution)/shard_map/ppermute | solution.py:94
  42.3 37.0 %collective-permute-start.8 = (bf16[96,832]{0,1:T(8,128)(2,1)}, bf16[96,832]{0,1:T(8,128)(2,1)}, u32[]{:S(2)}, u32[]{:S(2)}) collective-permute-start(bf16[96,832]{0,1:T(8,128)(2,1)} %pad_maximum_fusion.36), channel_id=1, source_target_pairs={{0,28},{4,24},{8,20},{12,16},{16,12},{20,8},{24,4},{28,0},{1,29},{... | collective-permute-start | bytes 479240 | tf_op jit(solution)/shard_map/ppermute | solution.py:94
  42.4 42.6 %collective-permute-start = (bf16[128,768]{1,0:T(8,128)(2,1)}, bf16[128,768]{1,0:T(8,128)(2,1)}, u32[]{:S(2)}, u32[]{:S(2)}) collective-permute-start(bf16[128,768]{1,0:T(8,128)(2,1)} %param.29), channel_id=1, source_target_pairs={{0,2},{2,0},{1,3},{3,1},{4,6},{6,4},{5,7},{7,5},{8,10},{10,8},{9,1... | collective-permute-start | bytes 589832 | tf_op jit(solution)/shard_map/ppermute | solution.py:89
  64.6 24.3 %collective-permute-start.12 = (bf16[96,1536]{1,0:T(8,128)(2,1)}, bf16[96,1536]{1,0:T(8,128)(2,1)S(1)}, u32[]{:S(2)}, u32[]{:S(2)}) collective-permute-start(bf16[96,1536]{1,0:T(8,128)(2,1)} %get-tuple-element.335), channel_id=1, source_target_pairs={{0,4},{4,0},{8,12},{12,8},{16,20},{20,16},{24,28},{28,24},{1,5},{5... | collective-permute-start | bytes 884744 | tf_op jit(solution)/shard_map/ppermute | solution.py:94
  69.0 20.7 %collective-permute-start.13 = (bf16[96,1536]{1,0:T(8,128)(2,1)}, bf16[96,1536]{1,0:T(8,128)(2,1)S(1)}, u32[]{:S(2)}, u32[]{:S(2)}) collective-permute-start(bf16[96,1536]{1,0:T(8,128)(2,1)} %get-tuple-element.335), channel_id=1, source_target_pairs={{0,8},{4,12},{8,0},{12,4},{16,24},{20,28},{24,16},{28,20},{1,9},{5... | collective-permute-start | bytes 884744 | tf_op jit(solution)/shard_map/ppermute | solution.py:94
  73.2 28.2 %collective-permute-start.14 = (bf16[96,1536]{1,0:T(8,128)(2,1)}, bf16[96,1536]{1,0:T(8,128)(2,1)}, u32[]{:S(2)}, u32[]{:S(2)}) collective-permute-start(bf16[96,1536]{1,0:T(8,128)(2,1)} %get-tuple-element.335), channel_id=1, source_target_pairs={{0,12},{4,8},{8,4},{12,0},{16,28},{20,24},{24,20},{28,16},{1,13},{... | collective-permute-start | bytes 884744 | tf_op jit(solution)/shard_map/ppermute | solution.py:94
  79.3 34.8 %collective-permute-start.15 = (bf16[96,1536]{1,0:T(8,128)(2,1)}, bf16[96,1536]{1,0:T(8,128)(2,1)}, u32[]{:S(2)}, u32[]{:S(2)}) collective-permute-start(bf16[96,1536]{1,0:T(8,128)(2,1)} %get-tuple-element.335), channel_id=1, source_target_pairs={{0,16},{4,20},{8,24},{12,28},{16,0},{20,4},{24,8},{28,12},{1,17},{... | collective-permute-start | bytes 884744 | tf_op jit(solution)/shard_map/ppermute | solution.py:94
  85.0 35.3 %collective-permute-start.16 = (bf16[96,1536]{1,0:T(8,128)(2,1)}, bf16[96,1536]{1,0:T(8,128)(2,1)S(1)}, u32[]{:S(2)}, u32[]{:S(2)}) collective-permute-start(bf16[96,1536]{1,0:T(8,128)(2,1)} %get-tuple-element.335), channel_id=1, source_target_pairs={{0,20},{4,16},{8,28},{12,24},{16,4},{20,0},{24,12},{28,8},{1,21},{... | collective-permute-start | bytes 884744 | tf_op jit(solution)/shard_map/ppermute | solution.py:94
  89.7 31.8 %collective-permute-start.17 = (bf16[96,1536]{1,0:T(8,128)(2,1)}, bf16[96,1536]{1,0:T(8,128)(2,1)S(1)}, u32[]{:S(2)}, u32[]{:S(2)}) collective-permute-start(bf16[96,1536]{1,0:T(8,128)(2,1)} %get-tuple-element.335), channel_id=1, source_target_pairs={{0,24},{4,28},{8,16},{12,20},{16,8},{20,12},{24,0},{28,4},{1,25},{... | collective-permute-start | bytes 884744 | tf_op jit(solution)/shard_map/ppermute | solution.py:94
  94.0 36.3 %collective-permute-start.18 = (bf16[96,1536]{1,0:T(8,128)(2,1)}, bf16[96,1536]{1,0:T(8,128)(2,1)S(1)}, u32[]{:S(2)}, u32[]{:S(2)}) collective-permute-start(bf16[96,1536]{1,0:T(8,128)(2,1)} %get-tuple-element.335), channel_id=1, source_target_pairs={{0,28},{4,24},{8,20},{12,16},{16,12},{20,8},{24,4},{28,0},{1,29},{... | collective-permute-start | bytes 884744 | tf_op jit(solution)/shard_map/ppermute | solution.py:94
  101.4 14.4 %collective-permute-start.9 = (bf16[256,768]{1,0:T(8,128)(2,1)S(1)}, bf16[256,768]{1,0:T(8,128)(2,1)S(1)}, u32[]{:S(2)}, u32[]{:S(2)}) collective-permute-start(bf16[256,768]{1,0:T(8,128)(2,1)S(1)} %slice.1295), channel_id=1, source_target_pairs={{0,1},{1,0},{2,3},{3,2},{4,5},{5,4},{6,7},{7,6},{8,9},{9,8},{10,11... | collective-permute-start | bytes 1179656 | tf_op jit(solution)/shard_map/ppermute | solution.py:85
  114.1 17.0 %collective-permute-start.34 = (bf16[1,768,1024]{2,1,0:T(8,128)(2,1)S(1)}, bf16[1,768,1024]{2,1,0:T(8,128)(2,1)S(1)}, u32[]{:S(2)}, u32[]{:S(2)}) collective-permute-start(bf16[1,768,1024]{2,1,0:T(8,128)(2,1)S(1)} %copy-done.55), channel_id=1, source_target_pairs={{0,1},{1,0},{2,3},{3,2},{4,5},{5,4},{6,7},{7,6},{8,9},{9,8},{10,11... | collective-permute-start | bytes 4718600 | tf_op jit(solution)/shard_map/ppermute | solution.py:85
  115.8 66.4 %collective-permute-start.35 = (bf16[1,768,512]{2,1,0:T(8,128)(2,1)}, bf16[1,768,512]{2,1,0:T(8,128)(2,1)}, u32[]{:S(2)}, u32[]{:S(2)}) collective-permute-start(bf16[1,768,512]{2,1,0:T(8,128)(2,1)} %get-tuple-element.295), channel_id=1, source_target_pairs={{0,1},{1,0},{2,3},{3,2},{4,5},{5,4},{6,7},{7,6},{8,9},{9,8},{10,11... | collective-permute-start | bytes 2359304 | tf_op jit(solution)/shard_map/ppermute | solution.py:85
  137.9 14.0 %collective-permute-start.20 = (bf16[64,768]{1,0:T(8,128)(2,1)}, bf16[64,768]{1,0:T(8,128)(2,1)}, u32[]{:S(2)}, u32[]{:S(2)}) collective-permute-start(bf16[64,768]{1,0:T(8,128)(2,1)} %get-tuple-element.315), channel_id=1, source_target_pairs={{0,8},{4,12},{8,0},{12,4},{16,24},{20,28},{24,16},{28,20},{1,9},{5... | collective-permute-start | bytes 294920 | tf_op jit(solution)/shard_map/ppermute | solution.py:94
  138.7 16.0 %collective-permute-start.21 = (bf16[64,768]{1,0:T(8,128)(2,1)}, bf16[64,768]{1,0:T(8,128)(2,1)}, u32[]{:S(2)}, u32[]{:S(2)}) collective-permute-start(bf16[64,768]{1,0:T(8,128)(2,1)} %get-tuple-element.314), channel_id=1, source_target_pairs={{0,12},{4,8},{8,4},{12,0},{16,28},{20,24},{24,20},{28,16},{1,13},{... | collective-permute-start | bytes 294920 | tf_op jit(solution)/shard_map/ppermute | solution.py:94
  139.8 17.5 %collective-permute-start.22 = (bf16[64,768]{1,0:T(8,128)(2,1)}, bf16[64,768]{1,0:T(8,128)(2,1)}, u32[]{:S(2)}, u32[]{:S(2)}) collective-permute-start(bf16[64,768]{1,0:T(8,128)(2,1)} %get-tuple-element.313), channel_id=1, source_target_pairs={{0,16},{4,20},{8,24},{12,28},{16,0},{20,4},{24,8},{28,12},{1,17},{... | collective-permute-start | bytes 294920 | tf_op jit(solution)/shard_map/ppermute | solution.py:94
  189.4 19.9 %collective-permute-start.44 = (bf16[2,1,64,768]{3,2,0,1:T(8,128)(2,1)S(1)}, bf16[2,1,64,768]{3,2,0,1:T(8,128)(2,1)S(1)}, u32[]{:S(2)}, u32[]{:S(2)}) collective-permute-start(bf16[2,1,64,768]{3,2,0,1:T(8,128)(2,1)S(1)} %slice_bitcast_fusion.38), channel_id=1, source_target_pairs={{0,2},{2,0},{1,3},{3,1},{4,6},{6,4},{5,7},{7,5},{8,10},{10,8},{9,1... | collective-permute-start | bytes 589832 | tf_op jit(solution)/shard_map/ppermute | solution.py:89
  227.2 15.0 %collective-permute-start.49 = (bf16[128,768]{1,0:T(8,128)(2,1)}, bf16[128,768]{1,0:T(8,128)(2,1)}, u32[]{:S(2)}, u32[]{:S(2)}) collective-permute-start(bf16[128,768]{1,0:T(8,128)(2,1)} %param.30), channel_id=1, source_target_pairs={{0,2},{2,0},{1,3},{3,1},{4,6},{6,4},{5,7},{7,5},{8,10},{10,8},{9,1... | collective-permute-start | bytes 589832 | tf_op jit(solution)/shard_map/ppermute | solution.py:89
  246.8 14.5 %collective-permute-start.50 = (bf16[256,768]{1,0:T(8,128)(2,1)}, bf16[256,768]{1,0:T(8,128)(2,1)}, u32[]{:S(2)}, u32[]{:S(2)}) collective-permute-start(bf16[256,768]{1,0:T(8,128)(2,1)} %multiply_convert_fusion.10), channel_id=1, source_target_pairs={{0,1},{1,0},{2,3},{3,2},{4,5},{5,4},{6,7},{7,6},{8,9},{9,8},{10,11... | collective-permute-start | bytes 1179656 | tf_op jit(solution)/shard_map/ppermute | solution.py:85
  265.3 17.3 %collective-permute-start.51 = (bf16[64,768]{1,0:T(8,128)(2,1)S(1)}, bf16[64,768]{1,0:T(8,128)(2,1)S(1)}, u32[]{:S(2)}, u32[]{:S(2)}) collective-permute-start(bf16[64,768]{1,0:T(8,128)(2,1)S(1)} %get-tuple-element.308), channel_id=1, source_target_pairs={{0,4},{4,0},{8,12},{12,8},{16,20},{20,16},{24,28},{28,24},{1,5},{5... | collective-permute-start | bytes 294920 | tf_op jit(solution)/shard_map/ppermute | solution.py:94
  265.9 19.0 %collective-permute-start.52 = (bf16[64,768]{1,0:T(8,128)(2,1)S(1)}, bf16[64,768]{1,0:T(8,128)(2,1)S(1)}, u32[]{:S(2)}, u32[]{:S(2)}) collective-permute-start(bf16[64,768]{1,0:T(8,128)(2,1)S(1)} %get-tuple-element.307), channel_id=1, source_target_pairs={{0,8},{4,12},{8,0},{12,4},{16,24},{20,28},{24,16},{28,20},{1,9},{5... | collective-permute-start | bytes 294920 | tf_op jit(solution)/shard_map/ppermute | solution.py:94
  268.6 18.8 %collective-permute-start.53 = (bf16[64,768]{1,0:T(8,128)(2,1)S(1)}, bf16[64,768]{1,0:T(8,128)(2,1)S(1)}, u32[]{:S(2)}, u32[]{:S(2)}) collective-permute-start(bf16[64,768]{1,0:T(8,128)(2,1)S(1)} %get-tuple-element.306), channel_id=1, source_target_pairs={{0,12},{4,8},{8,4},{12,0},{16,28},{20,24},{24,20},{28,16},{1,13},{... | collective-permute-start | bytes 294920 | tf_op jit(solution)/shard_map/ppermute | solution.py:94
  269.5 18.6 %collective-permute-start.54 = (bf16[64,768]{1,0:T(8,128)(2,1)S(1)}, bf16[64,768]{1,0:T(8,128)(2,1)S(1)}, u32[]{:S(2)}, u32[]{:S(2)}) collective-permute-start(bf16[64,768]{1,0:T(8,128)(2,1)S(1)} %get-tuple-element.305), channel_id=1, source_target_pairs={{0,16},{4,20},{8,24},{12,28},{16,0},{20,4},{24,8},{28,12},{1,17},{... | collective-permute-start | bytes 294920 | tf_op jit(solution)/shard_map/ppermute | solution.py:94
  271.6 17.9 %collective-permute-start.55 = (bf16[64,768]{1,0:T(8,128)(2,1)S(1)}, bf16[64,768]{1,0:T(8,128)(2,1)S(1)}, u32[]{:S(2)}, u32[]{:S(2)}) collective-permute-start(bf16[64,768]{1,0:T(8,128)(2,1)S(1)} %get-tuple-element.304), channel_id=1, source_target_pairs={{0,20},{4,16},{8,28},{12,24},{16,4},{20,0},{24,12},{28,8},{1,21},{... | collective-permute-start | bytes 294920 | tf_op jit(solution)/shard_map/ppermute | solution.py:94
  320.6 18.4 %collective-permute-start.74 = (bf16[2,1,64,768]{3,2,0,1:T(8,128)(2,1)S(1)}, bf16[2,1,64,768]{3,2,0,1:T(8,128)(2,1)S(1)}, u32[]{:S(2)}, u32[]{:S(2)}) collective-permute-start(bf16[2,1,64,768]{3,2,0,1:T(8,128)(2,1)S(1)} %slice_bitcast_fusion.30), channel_id=1, source_target_pairs={{0,2},{2,0},{1,3},{3,1},{4,6},{6,4},{5,7},{7,5},{8,10},{10,8},{9,1... | collective-permute-start | bytes 589832 | tf_op jit(solution)/shard_map/ppermute | solution.py:89
  369.8 30.9 %collective-permute-start.79 = (bf16[256,768]{1,0:T(8,128)(2,1)}, bf16[256,768]{1,0:T(8,128)(2,1)}, u32[]{:S(2)}, u32[]{:S(2)}) collective-permute-start(bf16[256,768]{1,0:T(8,128)(2,1)} %get-tuple-element.262), channel_id=1, source_target_pairs={{0,1},{1,0},{2,3},{3,2},{4,5},{5,4},{6,7},{7,6},{8,9},{9,8},{10,11... | collective-permute-start | bytes 1179656 | tf_op jit(solution)/shard_map/ppermute | solution.py:85
  400.3 33.1 %collective-permute-start.91 = (bf16[1,768,3,512]{3,1,2,0:T(8,128)(2,1)}, bf16[1,768,3,512]{3,1,2,0:T(8,128)(2,1)}, u32[]{:S(2)}, u32[]{:S(2)}) collective-permute-start(bf16[1,768,3,512]{3,1,2,0:T(8,128)(2,1)} %bitcast.427), channel_id=1, source_target_pairs={{0,1},{1,0},{2,3},{3,2},{4,5},{5,4},{6,7},{7,6},{8,9},{9,8},{10,11... | collective-permute-start | bytes 7077896 | tf_op jit(solution)/shard_map/ppermute | solution.py:85
  422.5 37.7 %all-to-all-start = ((bf16[8,96,832]{2,1,0:T(8,128)(2,1)}), bf16[8,96,832]{2,1,0:T(8,128)(2,1)S(1)}, u32[]{:S(2)}, u32[]{:S(2)}) async-start(bf16[8,96,832]{2,1,0:T(8,128)(2,1)} %bitcast.439), calls=%async_computation | async-start | bytes 2752512 | tf_op jit(solution)/shard_map/all_to_all | solution.py:141
  461.3 101.9 %all-to-all-start.1 = ((bf16[8,96,1536]{2,1,0:T(8,128)(2,1)}), bf16[8,96,1536]{2,1,0:T(8,128)(2,1)}, u32[]{:S(2)}, u32[]{:S(2)}) async-start(bf16[8,96,1536]{2,1,0:T(8,128)(2,1)} %pad_maximum_fusion.4), calls=%async_computation.1 | async-start | bytes 4718592 | tf_op jit(solution)/shard_map/all_to_all | solution.py:141
  465.7 200.2 %all-gather.2.cloned.1.call-start = ((), (), s32[]{:S(2)}) async-start(), calls=%async_computation.2 | async-start | bytes 2654208 | tf_op jit(solution)/shard_map/all_gather | solution.py:573
  499.2 28.8 %collective-permute-start.82 = (bf16[96,832]{0,1:T(8,128)(2,1)S(1)}, bf16[96,832]{0,1:T(8,128)(2,1)}, u32[]{:S(2)}, u32[]{:S(2)}) collective-permute-start(bf16[96,832]{0,1:T(8,128)(2,1)S(1)} %pad_maximum_fusion.37), channel_id=1, source_target_pairs={{0,12},{4,8},{8,4},{12,0},{16,28},{20,24},{24,20},{28,16},{1,13},{... | collective-permute-start | bytes 479240 | tf_op jit(solution)/shard_map/ppermute | solution.py:94
  499.5 44.4 %collective-permute-start.83 = (bf16[96,832]{0,1:T(8,128)(2,1)S(1)}, bf16[96,832]{0,1:T(8,128)(2,1)}, u32[]{:S(2)}, u32[]{:S(2)}) collective-permute-start(bf16[96,832]{0,1:T(8,128)(2,1)S(1)} %pad_maximum_fusion.37), channel_id=1, source_target_pairs={{0,16},{4,20},{8,24},{12,28},{16,0},{20,4},{24,8},{28,12},{1,17},{... | collective-permute-start | bytes 479240 | tf_op jit(solution)/shard_map/ppermute | solution.py:94
  502.2 47.0 %collective-permute-start.84 = (bf16[96,832]{0,1:T(8,128)(2,1)S(1)}, bf16[96,832]{0,1:T(8,128)(2,1)}, u32[]{:S(2)}, u32[]{:S(2)}) collective-permute-start(bf16[96,832]{0,1:T(8,128)(2,1)S(1)} %pad_maximum_fusion.37), channel_id=1, source_target_pairs={{0,20},{4,16},{8,28},{12,24},{16,4},{20,0},{24,12},{28,8},{1,21},{... | collective-permute-start | bytes 479240 | tf_op jit(solution)/shard_map/ppermute | solution.py:94
  505.8 47.1 %collective-permute-start.85 = (bf16[96,832]{0,1:T(8,128)(2,1)S(1)}, bf16[96,832]{0,1:T(8,128)(2,1)}, u32[]{:S(2)}, u32[]{:S(2)}) collective-permute-start(bf16[96,832]{0,1:T(8,128)(2,1)S(1)} %pad_maximum_fusion.37), channel_id=1, source_target_pairs={{0,24},{4,28},{8,16},{12,20},{16,8},{20,12},{24,0},{28,4},{1,25},{... | collective-permute-start | bytes 479240 | tf_op jit(solution)/shard_map/ppermute | solution.py:94
  510.3 46.3 %collective-permute-start.86 = (bf16[96,832]{0,1:T(8,128)(2,1)S(1)}, bf16[96,832]{0,1:T(8,128)(2,1)}, u32[]{:S(2)}, u32[]{:S(2)}) collective-permute-start(bf16[96,832]{0,1:T(8,128)(2,1)S(1)} %pad_maximum_fusion.37), channel_id=1, source_target_pairs={{0,28},{4,24},{8,20},{12,16},{16,12},{20,8},{24,4},{28,0},{1,29},{... | collective-permute-start | bytes 479240 | tf_op jit(solution)/shard_map/ppermute | solution.py:94
  528.0 47.3 %collective-permute-start.100 = (bf16[2,256,1536]{2,1,0:T(8,128)(2,1)}, bf16[2,256,1536]{2,1,0:T(8,128)(2,1)}, u32[]{:S(2)}, u32[]{:S(2)}) collective-permute-start(bf16[2,256,1536]{2,1,0:T(8,128)(2,1)} %broadcast_select_fusion.2), channel_id=1, source_target_pairs={{0,1},{1,0},{2,3},{3,2},{4,5},{5,4},{6,7},{7,6},{8,9},{9,8},{10,11... | collective-permute-start | bytes 4718600 | tf_op jit(solution)/shard_map/ppermute | solution.py:85
  581.6 63.7 %collective-permute-start.101 = (bf16[2,256,1536]{2,1,0:T(8,128)(2,1)S(1)}, bf16[2,256,1536]{2,1,0:T(8,128)(2,1)}, u32[]{:S(2)}, u32[]{:S(2)}) collective-permute-start(bf16[2,256,1536]{2,1,0:T(8,128)(2,1)S(1)} %copy-done.16), channel_id=1, source_target_pairs={{0,2},{2,0},{1,3},{3,1},{4,6},{6,4},{5,7},{7,5},{8,10},{10,8},{9,1... | collective-permute-start | bytes 4718600 | tf_op jit(solution)/shard_map/ppermute | solution.py:89
  586.5 48.0 %collective-permute-start.93 = (bf16[1,256,1536]{2,1,0:T(8,128)(2,1)S(1)}, bf16[1,256,1536]{2,1,0:T(8,128)(2,1)S(1)}, u32[]{:S(2)}, u32[]{:S(2)}) collective-permute-start(bf16[1,256,1536]{2,1,0:T(8,128)(2,1)S(1)} %add_convert_fusion.3.mine_ref), channel_id=1, source_target_pairs={{0,2},{2,0},{1,3},{3,1},{4,6},{6,4},{5,7},{7,5},{8,10},{10,8},{9,1... | collective-permute-start | bytes 2359304 | tf_op jit(solution)/shard_map/ppermute | solution.py:89
  642.9 16.1 %collective-permute-start.94 = (f32[1,8,128]{2,1,0:T(8,128)}, f32[1,8,128]{2,1,0:T(8,128)S(1)}, u32[]{:S(2)}, u32[]{:S(2)}) collective-permute-start(f32[1,8,128]{2,1,0:T(8,128)} %get-tuple-element.72), channel_id=1, source_target_pairs={{0,1},{1,0},{2,3},{3,2},{4,5},{5,4},{6,7},{7,6},{8,9},{9,8},{10,11... | collective-permute-start | bytes 12296 | tf_op jit(solution)/shard_map/ppermute | solution.py:85
  644.7 28.6 %collective-permute-start.95 = (bf16[1,768,768]{2,1,0:T(8,128)(2,1)}, bf16[1,768,768]{2,1,0:T(8,128)(2,1)}, u32[]{:S(2)}, u32[]{:S(2)}) collective-permute-start(bf16[1,768,768]{2,1,0:T(8,128)(2,1)} %get-tuple-element.73), channel_id=1, source_target_pairs={{0,1},{1,0},{2,3},{3,2},{4,5},{5,4},{6,7},{7,6},{8,9},{9,8},{10,11... | collective-permute-start | bytes 3538952 | tf_op jit(solution)/shard_map/ppermute | solution.py:85
  658.6 19.5 %collective-permute-start.103 = (bf16[2,768,768]{2,1,0:T(8,128)(2,1)}, bf16[2,768,768]{2,1,0:T(8,128)(2,1)}, u32[]{:S(2)}, u32[]{:S(2)}) collective-permute-start(bf16[2,768,768]{2,1,0:T(8,128)(2,1)} %get-tuple-element.77), channel_id=1, source_target_pairs={{0,1},{1,0},{2,3},{3,2},{4,5},{5,4},{6,7},{7,6},{8,9},{9,8},{10,11... | collective-permute-start | bytes 7077896 | tf_op jit(solution)/shard_map/ppermute | solution.py:85
  684.7 20.0 %collective-permute-start.97 = (bf16[1,256,1536]{2,1,0:T(8,128)(2,1)}, bf16[1,256,1536]{2,1,0:T(8,128)(2,1)}, u32[]{:S(2)}, u32[]{:S(2)}) collective-permute-start(bf16[1,256,1536]{2,1,0:T(8,128)(2,1)} %add_convert_fusion.2.mine_ref), channel_id=1, source_target_pairs={{0,2},{2,0},{1,3},{3,1},{4,6},{6,4},{5,7},{7,5},{8,10},{10,8},{9,1... | collective-permute-start | bytes 2359304 | tf_op jit(solution)/shard_map/ppermute | solution.py:89
  712.3 18.2 %collective-permute-start.99 = (bf16[1,768,768]{2,1,0:T(8,128)(2,1)}, bf16[1,768,768]{2,1,0:T(8,128)(2,1)S(1)}, u32[]{:S(2)}, u32[]{:S(2)}) collective-permute-start(bf16[1,768,768]{2,1,0:T(8,128)(2,1)} %get-tuple-element.75), channel_id=1, source_target_pairs={{0,1},{1,0},{2,3},{3,2},{4,5},{5,4},{6,7},{7,6},{8,9},{9,8},{10,11... | collective-permute-start | bytes 3538952 | tf_op jit(solution)/shard_map/ppermute | solution.py:85
  (254 other events, 1854.3 us)
Sparse Core Ops, SparseCore 0:
  568.0 50.2 all-gather.1
